TPU v7x, 256 devices: a whole 4x4x8 slice. The times are simulated.
256 devices in a mesh: win: 8 (over x, y_hi), col: 32 (over y_lo, z, core).
Axes of the slice: x: 4, y: 4 (y_hi: 2, y_lo: 2; y = y_hi * 2 + y_lo), z: 8, core: 2. Of those that a mesh axis runs over, the one named last changes fastest.
Arguments:
- increment: float32 [8, 32768, 128], P('win', 'col'), may hold values from -6 to 6
- dual_field: float32 [8, 32768, 128], P('win', 'col'), may hold values from -6 to 6
- departure: float32 [8, 32768, 128], P('win', 'col'), may hold values from -6 to 6
- obs_grad: float32 [8, 32768, 128], P('win', 'col'), may hold values from -6 to 6
- obs_weight: bfloat16 [8, 32768, 128], P('win', 'col'), may hold values from 0.099609375 to 4
- error_scale: float32 [8, 128], P('win'), may hold values from 0.4 to 1.6
- corr_blocks: bfloat16 [512, 64, 512], P('col')
- corr_pattern: int32 [512, 8], P('col'), may hold values from 0 to 511, as said below
- model_blocks: bfloat16 [512, 64, 256], P('col')
- model_pattern: int32 [512, 4], P('col'), may hold values from 0 to 511, as said below
Outputs:
- increment_next: float32 [8, 32768, 128], P('win', 'col')
- dual_next: float32 [8, 32768, 128], P('win', 'col')
Inputs may be any that keep to these rules, and one draw needn't show every extreme that they name: `corr_pattern`: each row i names distinct block columns within 4 blocks of i around the cycle of 512 blocks; slot 0 names i itself. `model_pattern`: each row i names distinct block columns within 2 blocks of i around the cycle of 512 blocks; slot 0 names i itself.
All inputs are finite; a program needn't handle non-finite values.
Results may differ from a plain program's by a relative error of at most 0.0046.
Values may be sent and summed in bfloat16 or wider, within the bound.
A program may use at most 64 MiB of HBM per device.

v0:
```python
import jax
import jax.numpy as jnp
from jax import lax
from jax.sharding import PartitionSpec as P

RU = 4
RM = 2


relax_factor = 0.75


def extended_2(value, sides, width):
    for axis, dim in sides:
        size, length = (lax.axis_size(axis), value.shape[dim])
        up = [(i, (i + 1) % size) for i in range(size)]
        down = [(j, i) for i, j in up]
        last = lax.slice_in_dim(value, length - width, length, axis=dim)
        first = lax.slice_in_dim(value, 0, width, axis=dim)
        before = lax.ppermute(last, axis, up)
        after = lax.ppermute(first, axis, down)
        value = jnp.concatenate([before, value, after], axis=dim)
    return value


def passed_along(value, axis, by):
    length = lax.axis_size(axis)
    pairs = [(i, i + by) for i in range(length) if 0 <= i + by < length]
    return lax.ppermute(value, axis, pairs)


def banded(blocks, pattern, reach_blocks):
    row_count, block_width, slot_count = (blocks.shape[0], blocks.shape[1], pattern.shape[1])
    total_blocks = row_count * lax.axis_size("col")
    own_rows = lax.axis_index("col") * row_count + jnp.arange(row_count, dtype=jnp.int32)
    position = (pattern - own_rows[:, None] + reach_blocks) % total_blocks
    selector = (
        position[:, :, None] == jnp.arange(2 * reach_blocks + 1, dtype=jnp.int32)[None, None, :]
    ).astype(jnp.bfloat16)
    split_blocks = blocks.reshape(row_count, block_width, slot_count, block_width)
    return jnp.einsum(
        "isp,iasc->iapc", selector, split_blocks, preferred_element_type=jnp.float32
    ).astype(jnp.bfloat16)


def band_product(band_blocks, extended, columns):
    row_count, block_width, band_count = (
        band_blocks.shape[0],
        band_blocks.shape[1],
        band_blocks.shape[2],
    )
    batch_depth, levels = (extended.shape[0], extended.shape[2])
    windows = jnp.stack(
        [
            extended[:, slot_index * block_width : slot_index * block_width + columns].reshape(
                batch_depth, row_count, block_width, levels
            )
            for slot_index in range(band_count)
        ],
        axis=2,
    )
    result = jnp.einsum(
        "iapc,sipcl->sial", band_blocks, windows, preferred_element_type=jnp.float32
    )
    return result.reshape(batch_depth, columns, levels)


def band_spread(band_blocks, field):
    row_count, block_width, band_count = (
        band_blocks.shape[0],
        band_blocks.shape[1],
        band_blocks.shape[2],
    )
    batch_depth, columns, levels = field.shape
    band_parts = jnp.einsum(
        "iapc,sial->sipcl",
        band_blocks,
        field.reshape(batch_depth, row_count, block_width, levels),
        preferred_element_type=jnp.float32,
    )
    spread_sum = jnp.zeros(
        (batch_depth, columns + (band_count - 1) * block_width, levels), jnp.float32
    )
    for slot_index in range(band_count):
        term_part = band_parts[:, :, slot_index].reshape(batch_depth, columns, levels)
        spread_sum = spread_sum.at[
            :, slot_index * block_width : slot_index * block_width + columns
        ].add(term_part)
    return spread_sum


def settle(spread_sum, arrived, rim_width):
    middle = spread_sum[:, rim_width : spread_sum.shape[1] - rim_width]
    middle = middle.at[:, :rim_width].add(arrived[:, :rim_width])
    return middle.at[:, middle.shape[1] - rim_width :].add(
        arrived[:, arrived.shape[1] - rim_width :]
    )


def rim_rows(spread_sum, rim_width):
    return jnp.concatenate(
        [spread_sum[:, :rim_width], spread_sum[:, spread_sum.shape[1] - rim_width :]], axis=1
    )


def corr_forward(band_blocks, field):
    rim_width = RU * band_blocks.shape[1]
    extended = extended_2(field, (("col", 1),), rim_width)
    return band_product(band_blocks, extended, field.shape[1])


def corr_adjoint(band_blocks, field):
    rim_width = RU * band_blocks.shape[1]
    spread_sum = band_spread(band_blocks, field)
    arrived = extended_2(rim_rows(spread_sum, rim_width), (("col", 1),), rim_width)
    return settle(spread_sum, arrived, rim_width)


def model_forward(band_blocks, field):
    rim_width = RM * band_blocks.shape[1]
    extended = extended_2(field, (("col", 1),), rim_width)
    return band_product(band_blocks, extended, field.shape[1])


def model_adjoint(band_blocks, field):
    rim_width = RM * band_blocks.shape[1]
    spread_sum = band_spread(band_blocks, field)
    arrived = extended_2(rim_rows(spread_sum, rim_width), (("col", 1),), rim_width)
    return settle(spread_sum, arrived, rim_width)


def body(
    increment,
    dual_field,
    departure,
    obs_grad,
    obs_weight,
    error_scale,
    corr_blocks,
    corr_pattern,
    model_blocks,
    model_pattern,
):
    corr_band = banded(corr_blocks, corr_pattern, RU)
    model_band = banded(model_blocks, model_pattern, RM)
    scaling = error_scale[:, None, :]
    local_count = increment.shape[0]
    win_count = lax.axis_size("win")

    def covariance(field):
        scaled = (scaling * field).astype(jnp.bfloat16)
        inner_term = corr_adjoint(corr_band, scaled).astype(jnp.bfloat16)
        return scaling * corr_forward(corr_band, inner_term)

    advanced = model_forward(model_band, increment.astype(jnp.bfloat16))
    carried = passed_along(advanced[local_count - 1], "win", 1)
    before = jnp.concatenate([carried[None], advanced[: local_count - 1]], axis=0)
    resid_dual = departure - covariance(dual_field) - (increment - before)
    pulled = model_adjoint(model_band, dual_field.astype(jnp.bfloat16))
    later_term = passed_along(pulled[0], "win", -1)
    after_terms = jnp.concatenate([pulled[1:], later_term[None]], axis=0)
    resid_incr = obs_weight.astype(jnp.float32) * increment - obs_grad - (dual_field - after_terms)

    def back_turn(turn_index, relay_state):
        incoming, held_states = relay_state
        running = resid_incr[local_count - 1] + model_adjoint(model_band, incoming[None])[0]
        fresh_states = [running]
        held_states = jnp.stack(fresh_states)
        incoming = passed_along(held_states[0].astype(jnp.bfloat16), "win", -1)
        return (incoming, held_states)

    initial = (jnp.zeros(resid_incr.shape[1:], jnp.bfloat16), jnp.zeros_like(resid_incr))
    step_dual = lax.fori_loop(0, win_count, back_turn, initial)[1]
    target = resid_dual - covariance(step_dual)

    def fore_turn(turn_index, relay_state):
        incoming, held_states = relay_state
        running = target[0] + model_forward(model_band, incoming[None])[0]
        fresh_states = [running]
        held_states = jnp.stack(fresh_states)
        incoming = passed_along(held_states[local_count - 1].astype(jnp.bfloat16), "win", 1)
        return (incoming, held_states)

    initial = (jnp.zeros(target.shape[1:], jnp.bfloat16), jnp.zeros_like(target))
    step_incr = lax.fori_loop(0, win_count, fore_turn, initial)[1]
    return (increment + relax_factor * step_incr, dual_field + relax_factor * step_dual)


def solution(mesh):
    return jax.shard_map(
        body,
        mesh=mesh,
        in_specs=(
            P("win", "col", None),
            P("win", "col", None),
            P("win", "col", None),
            P("win", "col", None),
            P("win", "col", None),
            P("win", None),
            P("col", None, None),
            P("col", None),
            P("col", None, None),
            P("col", None),
        ),
        out_specs=(P("win", "col", None), P("win", "col", None)),
        check_vma=False,
    )
```

profile of v0, /device:TPU:6, one launch (start us, length us, event | category | flops | bytes accessed | tf_op | source)
XLA Modules:
  0.0 401.6 jit_solution(17383880007164773698)
XLA Ops:
  10.6 8.2 %collective-permute-done.13 = f32[1,128,128]{2,1,0:T(8,128)S(1)} collective-permute-done((f32[1,128,128]{2,1,0:T(8,128)S(1)}, f32[1,128,128]{2,1,0:T(8,128)S(1)}, u32[]{:S(2)}, u32[]{:S(2)}) %collective-permute-start.13) | collective-permute-done | bytes 65568 | tf_op jit(solution)/shard_map/ppermute | solution.py:20
  35.7 6.1 %copy.13 = bf16[16,64,9,64]{1,3,2,0:T(8,128)(2,1)} copy(bf16[16,64,9,64]{3,2,1,0:T(8,128)(2,1)} %convert_bitcast_fusion) | data formatting | bytes 2359296 | tf_op jit(solution)/shard_map/convert_element_type | solution.py:43
  45.2 175.1 %while.63 = (s32[]{:T(128)}, bf16[1024,128]{1,0:T(8,128)(2,1)S(1)}, f32[1,1024,128]{2,1,0:T(8,128)}, f32[1,1024,128]{2,1,0:T(8,128)S(1)}, bf16[16,64,5,64]{1,3,2,0:T(8,128)(2,1)S(1)}, /*index=5*/s32[]{:T(128)}, f32[]{:T(128)}) while((s32[]{:T(128)}, bf16[1024,128]{1,0:T(8,128)(2,1)S(1)}, f32[1,1024,128]{2,1,0:T(8,128)}, ...), condition=%wide.region_1.2_spmd, body=%wide.region_0.1_spmd.sunk | while | flops 84705280 | bytes 22937800 | solution.py:173
  46.7 5.7 %collective-permute-done = f32[1,128,128]{2,1,0:T(8,128)S(1)} collective-permute-done((f32[1,128,128]{2,1,0:T(8,128)S(1)}, f32[1,128,128]{2,1,0:T(8,128)S(1)}, u32[]{:S(2)}, u32[]{:S(2)}) %collective-permute-start) | collective-permute-done | bytes 65568 | tf_op jit(solution)/shard_map/while/body/eval_jaxpr/ppermute | solution.py:20
  58.3 8.4 %collective-permute-done.2 = bf16[1024,128]{1,0:T(8,128)(2,1)S(1)} collective-permute-done((bf16[1024,128]{1,0:T(8,128)(2,1)}, bf16[1024,128]{1,0:T(8,128)(2,1)S(1)}, u32[]{:S(2)}, u32[]{:S(2)}) %collective-permute-start.2) | collective-permute-done | bytes 262176 | tf_op jit(solution)/shard_map/while/body/eval_jaxpr/ppermute | solution.py:29
  68.1 5.7 %collective-permute-done = f32[1,128,128]{2,1,0:T(8,128)S(1)} collective-permute-done((f32[1,128,128]{2,1,0:T(8,128)S(1)}, f32[1,128,128]{2,1,0:T(8,128)S(1)}, u32[]{:S(2)}, u32[]{:S(2)}) %collective-permute-start) | collective-permute-done | bytes 65568 | tf_op jit(solution)/shard_map/while/body/eval_jaxpr/ppermute | solution.py:20
  80.7 7.5 %collective-permute-done.2 = bf16[1024,128]{1,0:T(8,128)(2,1)S(1)} collective-permute-done((bf16[1024,128]{1,0:T(8,128)(2,1)}, bf16[1024,128]{1,0:T(8,128)(2,1)S(1)}, u32[]{:S(2)}, u32[]{:S(2)}) %collective-permute-start.2) | collective-permute-done | bytes 262176 | tf_op jit(solution)/shard_map/while/body/eval_jaxpr/ppermute | solution.py:29
  89.6 5.7 %collective-permute-done = f32[1,128,128]{2,1,0:T(8,128)S(1)} collective-permute-done((f32[1,128,128]{2,1,0:T(8,128)S(1)}, f32[1,128,128]{2,1,0:T(8,128)S(1)}, u32[]{:S(2)}, u32[]{:S(2)}) %collective-permute-start) | collective-permute-done | bytes 65568 | tf_op jit(solution)/shard_map/while/body/eval_jaxpr/ppermute | solution.py:20
  103.0 6.6 %collective-permute-done.2 = bf16[1024,128]{1,0:T(8,128)(2,1)S(1)} collective-permute-done((bf16[1024,128]{1,0:T(8,128)(2,1)}, bf16[1024,128]{1,0:T(8,128)(2,1)S(1)}, u32[]{:S(2)}, u32[]{:S(2)}) %collective-permute-start.2) | collective-permute-done | bytes 262176 | tf_op jit(solution)/shard_map/while/body/eval_jaxpr/ppermute | solution.py:29
  132.5 5.7 %collective-permute-done = f32[1,128,128]{2,1,0:T(8,128)S(1)} collective-permute-done((f32[1,128,128]{2,1,0:T(8,128)S(1)}, f32[1,128,128]{2,1,0:T(8,128)S(1)}, u32[]{:S(2)}, u32[]{:S(2)}) %collective-permute-start) | collective-permute-done | bytes 65568 | tf_op jit(solution)/shard_map/while/body/eval_jaxpr/ppermute | solution.py:20
  141.2 6.5 %collective-permute-start.2 = (bf16[1024,128]{1,0:T(8,128)(2,1)}, bf16[1024,128]{1,0:T(8,128)(2,1)S(1)}, u32[]{:S(2)}, u32[]{:S(2)}) collective-permute-start(bf16[1024,128]{1,0:T(8,128)(2,1)} %get-tuple-element.764), channel_id=1, source_target_pairs={{32,0},{64,32},{96,64},{128,96},{160,128},{192,160},{224,192},{33,... | collective-permute-start | bytes 786440 | tf_op jit(solution)/shard_map/while/body/eval_jaxpr/ppermute | solution.py:29
  154.7 5.7 %collective-permute-done = f32[1,128,128]{2,1,0:T(8,128)S(1)} collective-permute-done((f32[1,128,128]{2,1,0:T(8,128)S(1)}, f32[1,128,128]{2,1,0:T(8,128)S(1)}, u32[]{:S(2)}, u32[]{:S(2)}) %collective-permute-start) | collective-permute-done | bytes 65568 | tf_op jit(solution)/shard_map/while/body/eval_jaxpr/ppermute | solution.py:20
  163.4 6.7 %collective-permute-start.2 = (bf16[1024,128]{1,0:T(8,128)(2,1)}, bf16[1024,128]{1,0:T(8,128)(2,1)S(1)}, u32[]{:S(2)}, u32[]{:S(2)}) collective-permute-start(bf16[1024,128]{1,0:T(8,128)(2,1)} %get-tuple-element.764), channel_id=1, source_target_pairs={{32,0},{64,32},{96,64},{128,96},{160,128},{192,160},{224,192},{33,... | collective-permute-start | bytes 786440 | tf_op jit(solution)/shard_map/while/body/eval_jaxpr/ppermute | solution.py:29
  185.7 6.7 %collective-permute-start.2 = (bf16[1024,128]{1,0:T(8,128)(2,1)}, bf16[1024,128]{1,0:T(8,128)(2,1)S(1)}, u32[]{:S(2)}, u32[]{:S(2)}) collective-permute-start(bf16[1024,128]{1,0:T(8,128)(2,1)} %get-tuple-element.764), channel_id=1, source_target_pairs={{32,0},{64,32},{96,64},{128,96},{160,128},{192,160},{224,192},{33,... | collective-permute-start | bytes 786440 | tf_op jit(solution)/shard_map/while/body/eval_jaxpr/ppermute | solution.py:29
  208.1 6.7 %collective-permute-start.2 = (bf16[1024,128]{1,0:T(8,128)(2,1)}, bf16[1024,128]{1,0:T(8,128)(2,1)S(1)}, u32[]{:S(2)}, u32[]{:S(2)}) collective-permute-start(bf16[1024,128]{1,0:T(8,128)(2,1)} %get-tuple-element.764), channel_id=1, source_target_pairs={{32,0},{64,32},{96,64},{128,96},{160,128},{192,160},{224,192},{33,... | collective-permute-start | bytes 786440 | tf_op jit(solution)/shard_map/while/body/eval_jaxpr/ppermute | solution.py:29
  257.6 142.1 %while.64 = (s32[]{:T(128)}, bf16[1024,128]{1,0:T(8,128)(2,1)S(1)}, f32[1,1024,128]{2,1,0:T(8,128)}, f32[1,1024,128]{2,1,0:T(8,128)S(1)}, bf16[16,64,5,64]{3,1,2,0:T(8,128)(2,1)S(1)}, /*index=5*/s32[]{:T(128)}) while((s32[]{:T(128)}, bf16[1024,128]{1,0:T(8,128)(2,1)S(1)}, f32[1,1024,128]{2,1,0:T(8,128)}, f32[1,1024,128]{2,1,0:T(8,128)S(1)}, ...), condition=%wide.region_3.4_spmd, body=%wide.region_2.3_spmd.sunk | while | flops 86376448 | bytes 10813629 | solution.py:185
  270.7 9.3 %collective-permute-done.5 = bf16[1024,128]{1,0:T(8,128)(2,1)S(1)} collective-permute-done((bf16[1024,128]{1,0:T(8,128)(2,1)S(1)}, bf16[1024,128]{1,0:T(8,128)(2,1)S(1)}, u32[]{:S(2)}, u32[]{:S(2)}) %collective-permute-start.5) | collective-permute-done | bytes 262176 | tf_op jit(solution)/shard_map/while/body/eval_jaxpr/ppermute | solution.py:29
  289.2 7.9 %collective-permute-done.5 = bf16[1024,128]{1,0:T(8,128)(2,1)S(1)} collective-permute-done((bf16[1024,128]{1,0:T(8,128)(2,1)S(1)}, bf16[1024,128]{1,0:T(8,128)(2,1)S(1)}, u32[]{:S(2)}, u32[]{:S(2)}) %collective-permute-start.5) | collective-permute-done | bytes 262176 | tf_op jit(solution)/shard_map/while/body/eval_jaxpr/ppermute | solution.py:29
  306.3 7.9 %collective-permute-done.5 = bf16[1024,128]{1,0:T(8,128)(2,1)S(1)} collective-permute-done((bf16[1024,128]{1,0:T(8,128)(2,1)S(1)}, bf16[1024,128]{1,0:T(8,128)(2,1)S(1)}, u32[]{:S(2)}, u32[]{:S(2)}) %collective-permute-start.5) | collective-permute-done | bytes 262176 | tf_op jit(solution)/shard_map/while/body/eval_jaxpr/ppermute | solution.py:29
  323.4 7.9 %collective-permute-done.5 = bf16[1024,128]{1,0:T(8,128)(2,1)S(1)} collective-permute-done((bf16[1024,128]{1,0:T(8,128)(2,1)S(1)}, bf16[1024,128]{1,0:T(8,128)(2,1)S(1)}, u32[]{:S(2)}, u32[]{:S(2)}) %collective-permute-start.5) | collective-permute-done | bytes 262176 | tf_op jit(solution)/shard_map/while/body/eval_jaxpr/ppermute | solution.py:29
  340.5 7.9 %collective-permute-done.5 = bf16[1024,128]{1,0:T(8,128)(2,1)S(1)} collective-permute-done((bf16[1024,128]{1,0:T(8,128)(2,1)S(1)}, bf16[1024,128]{1,0:T(8,128)(2,1)S(1)}, u32[]{:S(2)}, u32[]{:S(2)}) %collective-permute-start.5) | collective-permute-done | bytes 262176 | tf_op jit(solution)/shard_map/while/body/eval_jaxpr/ppermute | solution.py:29
  357.6 7.9 %collective-permute-done.5 = bf16[1024,128]{1,0:T(8,128)(2,1)S(1)} collective-permute-done((bf16[1024,128]{1,0:T(8,128)(2,1)S(1)}, bf16[1024,128]{1,0:T(8,128)(2,1)S(1)}, u32[]{:S(2)}, u32[]{:S(2)}) %collective-permute-start.5) | collective-permute-done | bytes 262176 | tf_op jit(solution)/shard_map/while/body/eval_jaxpr/ppermute | solution.py:29
  374.7 7.9 %collective-permute-done.5 = bf16[1024,128]{1,0:T(8,128)(2,1)S(1)} collective-permute-done((bf16[1024,128]{1,0:T(8,128)(2,1)S(1)}, bf16[1024,128]{1,0:T(8,128)(2,1)S(1)}, u32[]{:S(2)}, u32[]{:S(2)}) %collective-permute-start.5) | collective-permute-done | bytes 262176 | tf_op jit(solution)/shard_map/while/body/eval_jaxpr/ppermute | solution.py:29
  391.8 7.9 %collective-permute-done.5 = bf16[1024,128]{1,0:T(8,128)(2,1)S(1)} collective-permute-done((bf16[1024,128]{1,0:T(8,128)(2,1)S(1)}, bf16[1024,128]{1,0:T(8,128)(2,1)S(1)}, u32[]{:S(2)}, u32[]{:S(2)}) %collective-permute-start.5) | collective-permute-done | bytes 262176 | tf_op jit(solution)/shard_map/while/body/eval_jaxpr/ppermute | solution.py:29
  (401 shorter events, 242.1 us)
Async XLA Ops:
  10.5 8.3 %collective-permute-start.13 = (f32[1,128,128]{2,1,0:T(8,128)S(1)}, f32[1,128,128]{2,1,0:T(8,128)S(1)}, u32[]{:S(2)}, u32[]{:S(2)}) collective-permute-start(f32[1,128,128]{2,1,0:T(8,128)S(1)} %slice.1304), channel_id=1, source_target_pairs={{0,1},{1,2},{2,3},{3,4},{4,5},{5,6},{6,7},{7,8},{8,9},{9,10},{10,1... | collective-permute-start | bytes 196616 | tf_op jit(solution)/shard_map/ppermute | solution.py:20
  21.5 20.3 %collective-permute-start.15 = (f32[1024,128]{1,0:T(8,128)}, f32[1024,128]{1,0:T(8,128)}, u32[]{:S(2)}, u32[]{:S(2)}) collective-permute-start(f32[1024,128]{1,0:T(8,128)} %fusion.54), channel_id=1, source_target_pairs={{32,0},{64,32},{96,64},{128,96},{160,128},{192,160},{224,192},{33,... | collective-permute-start | bytes 1572872 | tf_op jit(solution)/shard_map/ppermute | solution.py:29
  55.4 11.3 %collective-permute-start.2 = (bf16[1024,128]{1,0:T(8,128)(2,1)}, bf16[1024,128]{1,0:T(8,128)(2,1)S(1)}, u32[]{:S(2)}, u32[]{:S(2)}) collective-permute-start(bf16[1024,128]{1,0:T(8,128)(2,1)} %get-tuple-element.764), channel_id=1, source_target_pairs={{32,0},{64,32},{96,64},{128,96},{160,128},{192,160},{224,192},{33,... | collective-permute-start | bytes 786440 | tf_op jit(solution)/shard_map/while/body/eval_jaxpr/ppermute | solution.py:29
  76.8 11.3 %collective-permute-start.2 = (bf16[1024,128]{1,0:T(8,128)(2,1)}, bf16[1024,128]{1,0:T(8,128)(2,1)S(1)}, u32[]{:S(2)}, u32[]{:S(2)}) collective-permute-start(bf16[1024,128]{1,0:T(8,128)(2,1)} %get-tuple-element.764), channel_id=1, source_target_pairs={{32,0},{64,32},{96,64},{128,96},{160,128},{192,160},{224,192},{33,... | collective-permute-start | bytes 786440 | tf_op jit(solution)/shard_map/while/body/eval_jaxpr/ppermute | solution.py:29
  98.3 11.3 %collective-permute-start.2 = (bf16[1024,128]{1,0:T(8,128)(2,1)}, bf16[1024,128]{1,0:T(8,128)(2,1)S(1)}, u32[]{:S(2)}, u32[]{:S(2)}) collective-permute-start(bf16[1024,128]{1,0:T(8,128)(2,1)} %get-tuple-element.764), channel_id=1, source_target_pairs={{32,0},{64,32},{96,64},{128,96},{160,128},{192,160},{224,192},{33,... | collective-permute-start | bytes 786440 | tf_op jit(solution)/shard_map/while/body/eval_jaxpr/ppermute | solution.py:29
  119.7 11.3 %collective-permute-start.2 = (bf16[1024,128]{1,0:T(8,128)(2,1)}, bf16[1024,128]{1,0:T(8,128)(2,1)S(1)}, u32[]{:S(2)}, u32[]{:S(2)}) collective-permute-start(bf16[1024,128]{1,0:T(8,128)(2,1)} %get-tuple-element.764), channel_id=1, source_target_pairs={{32,0},{64,32},{96,64},{128,96},{160,128},{192,160},{224,192},{33,... | collective-permute-start | bytes 786440 | tf_op jit(solution)/shard_map/while/body/eval_jaxpr/ppermute | solution.py:29
  141.2 12.0 %collective-permute-start.2 = (bf16[1024,128]{1,0:T(8,128)(2,1)}, bf16[1024,128]{1,0:T(8,128)(2,1)S(1)}, u32[]{:S(2)}, u32[]{:S(2)}) collective-permute-start(bf16[1024,128]{1,0:T(8,128)(2,1)} %get-tuple-element.764), channel_id=1, source_target_pairs={{32,0},{64,32},{96,64},{128,96},{160,128},{192,160},{224,192},{33,... | collective-permute-start | bytes 786440 | tf_op jit(solution)/shard_map/while/body/eval_jaxpr/ppermute | solution.py:29
  163.4 12.2 %collective-permute-start.2 = (bf16[1024,128]{1,0:T(8,128)(2,1)}, bf16[1024,128]{1,0:T(8,128)(2,1)S(1)}, u32[]{:S(2)}, u32[]{:S(2)}) collective-permute-start(bf16[1024,128]{1,0:T(8,128)(2,1)} %get-tuple-element.764), channel_id=1, source_target_pairs={{32,0},{64,32},{96,64},{128,96},{160,128},{192,160},{224,192},{33,... | collective-permute-start | bytes 786440 | tf_op jit(solution)/shard_map/while/body/eval_jaxpr/ppermute | solution.py:29
  185.7 12.2 %collective-permute-start.2 = (bf16[1024,128]{1,0:T(8,128)(2,1)}, bf16[1024,128]{1,0:T(8,128)(2,1)S(1)}, u32[]{:S(2)}, u32[]{:S(2)}) collective-permute-start(bf16[1024,128]{1,0:T(8,128)(2,1)} %get-tuple-element.764), channel_id=1, source_target_pairs={{32,0},{64,32},{96,64},{128,96},{160,128},{192,160},{224,192},{33,... | collective-permute-start | bytes 786440 | tf_op jit(solution)/shard_map/while/body/eval_jaxpr/ppermute | solution.py:29
  208.1 12.2 %collective-permute-start.2 = (bf16[1024,128]{1,0:T(8,128)(2,1)}, bf16[1024,128]{1,0:T(8,128)(2,1)S(1)}, u32[]{:S(2)}, u32[]{:S(2)}) collective-permute-start(bf16[1024,128]{1,0:T(8,128)(2,1)} %get-tuple-element.764), channel_id=1, source_target_pairs={{32,0},{64,32},{96,64},{128,96},{160,128},{192,160},{224,192},{33,... | collective-permute-start | bytes 786440 | tf_op jit(solution)/shard_map/while/body/eval_jaxpr/ppermute | solution.py:29
  226.6 11.2 %collective-permute-start.6 = (f32[1,256,128]{2,1,0:T(8,128)S(1)}, f32[1,256,128]{2,1,0:T(8,128)S(1)}, u32[]{:S(2)}, u32[]{:S(2)}) collective-permute-start(f32[1,256,128]{2,1,0:T(8,128)S(1)} %slice.1271), channel_id=1, source_target_pairs={{0,1},{1,2},{2,3},{3,4},{4,5},{5,6},{6,7},{7,8},{8,9},{9,10},{10,1... | collective-permute-start | bytes 393224 | tf_op jit(solution)/shard_map/ppermute | solution.py:20
  234.5 7.3 %collective-permute-start.16 = (f32[1,256,128]{2,1,0:T(8,128)S(1)}, f32[1,256,128]{2,1,0:T(8,128)S(1)}, u32[]{:S(2)}, u32[]{:S(2)}) collective-permute-start(f32[1,256,128]{2,1,0:T(8,128)S(1)} %slice.1325), channel_id=1, source_target_pairs={{0,1},{1,2},{2,3},{3,4},{4,5},{5,6},{6,7},{7,8},{8,9},{9,10},{10,1... | collective-permute-start | bytes 393224 | tf_op jit(solution)/shard_map/ppermute | solution.py:20
  235.9 20.4 %collective-permute-start.12 = (f32[1024,128]{1,0:T(8,128)S(1)}, f32[1024,128]{1,0:T(8,128)S(1)}, u32[]{:S(2)}, u32[]{:S(2)}) collective-permute-start(f32[1024,128]{1,0:T(8,128)S(1)} %bitcast.316), channel_id=1, source_target_pairs={{0,32},{32,64},{64,96},{96,128},{128,160},{160,192},{192,224},{1,3... | collective-permute-start | bytes 1572872 | tf_op jit(solution)/shard_map/ppermute | solution.py:29
  241.8 6.9 %collective-permute-start.17 = (f32[1,256,128]{2,1,0:T(8,128)S(1)}, f32[1,256,128]{2,1,0:T(8,128)S(1)}, u32[]{:S(2)}, u32[]{:S(2)}) collective-permute-start(f32[1,256,128]{2,1,0:T(8,128)S(1)} %get-tuple-element.633), channel_id=1, source_target_pairs={{1,0},{2,1},{3,2},{4,3},{5,4},{6,5},{7,6},{8,7},{9,8},{10,9},{11,1... | collective-permute-start | bytes 393224 | tf_op jit(solution)/shard_map/ppermute | solution.py:21
  244.4 8.3 %collective-permute-start.8 = (bf16[1,256,128]{2,1,0:T(8,128)(2,1)S(1)}, bf16[1,256,128]{2,1,0:T(8,128)(2,1)S(1)}, u32[]{:S(2)}, u32[]{:S(2)}) collective-permute-start(bf16[1,256,128]{2,1,0:T(8,128)(2,1)S(1)} %get-tuple-element.667), channel_id=1, source_target_pairs={{0,1},{1,2},{2,3},{3,4},{4,5},{5,6},{6,7},{7,8},{8,9},{9,10},{10,1... | collective-permute-start | bytes 196616 | tf_op jit(solution)/shard_map/ppermute | solution.py:20
  244.5 8.2 %collective-permute-start.9 = (bf16[1,256,128]{2,1,0:T(8,128)(2,1)S(1)}, bf16[1,256,128]{2,1,0:T(8,128)(2,1)S(1)}, u32[]{:S(2)}, u32[]{:S(2)}) collective-permute-start(bf16[1,256,128]{2,1,0:T(8,128)(2,1)S(1)} %get-tuple-element.666), channel_id=1, source_target_pairs={{1,0},{2,1},{3,2},{4,3},{5,4},{6,5},{7,6},{8,7},{9,8},{10,9},{11,1... | collective-permute-start | bytes 196616 | tf_op jit(solution)/shard_map/ppermute | solution.py:21
  267.9 12.1 %collective-permute-start.5 = (bf16[1024,128]{1,0:T(8,128)(2,1)S(1)}, bf16[1024,128]{1,0:T(8,128)(2,1)S(1)}, u32[]{:S(2)}, u32[]{:S(2)}) collective-permute-start(bf16[1024,128]{1,0:T(8,128)(2,1)S(1)} %fusion.120), channel_id=1, source_target_pairs={{0,32},{32,64},{64,96},{96,128},{128,160},{160,192},{192,224},{1,3... | collective-permute-start | bytes 786440 | tf_op jit(solution)/shard_map/while/body/eval_jaxpr/ppermute | solution.py:29
  286.4 10.7 %collective-permute-start.5 = (bf16[1024,128]{1,0:T(8,128)(2,1)S(1)}, bf16[1024,128]{1,0:T(8,128)(2,1)S(1)}, u32[]{:S(2)}, u32[]{:S(2)}) collective-permute-start(bf16[1024,128]{1,0:T(8,128)(2,1)S(1)} %fusion.120), channel_id=1, source_target_pairs={{0,32},{32,64},{64,96},{96,128},{128,160},{160,192},{192,224},{1,3... | collective-permute-start | bytes 786440 | tf_op jit(solution)/shard_map/while/body/eval_jaxpr/ppermute | solution.py:29
  303.5 10.7 %collective-permute-start.5 = (bf16[1024,128]{1,0:T(8,128)(2,1)S(1)}, bf16[1024,128]{1,0:T(8,128)(2,1)S(1)}, u32[]{:S(2)}, u32[]{:S(2)}) collective-permute-start(bf16[1024,128]{1,0:T(8,128)(2,1)S(1)} %fusion.120), channel_id=1, source_target_pairs={{0,32},{32,64},{64,96},{96,128},{128,160},{160,192},{192,224},{1,3... | collective-permute-start | bytes 786440 | tf_op jit(solution)/shard_map/while/body/eval_jaxpr/ppermute | solution.py:29
  320.6 10.7 %collective-permute-start.5 = (bf16[1024,128]{1,0:T(8,128)(2,1)S(1)}, bf16[1024,128]{1,0:T(8,128)(2,1)S(1)}, u32[]{:S(2)}, u32[]{:S(2)}) collective-permute-start(bf16[1024,128]{1,0:T(8,128)(2,1)S(1)} %fusion.120), channel_id=1, source_target_pairs={{0,32},{32,64},{64,96},{96,128},{128,160},{160,192},{192,224},{1,3... | collective-permute-start | bytes 786440 | tf_op jit(solution)/shard_map/while/body/eval_jaxpr/ppermute | solution.py:29
  337.7 10.7 %collective-permute-start.5 = (bf16[1024,128]{1,0:T(8,128)(2,1)S(1)}, bf16[1024,128]{1,0:T(8,128)(2,1)S(1)}, u32[]{:S(2)}, u32[]{:S(2)}) collective-permute-start(bf16[1024,128]{1,0:T(8,128)(2,1)S(1)} %fusion.120), channel_id=1, source_target_pairs={{0,32},{32,64},{64,96},{96,128},{128,160},{160,192},{192,224},{1,3... | collective-permute-start | bytes 786440 | tf_op jit(solution)/shard_map/while/body/eval_jaxpr/ppermute | solution.py:29
  354.8 10.7 %collective-permute-start.5 = (bf16[1024,128]{1,0:T(8,128)(2,1)S(1)}, bf16[1024,128]{1,0:T(8,128)(2,1)S(1)}, u32[]{:S(2)}, u32[]{:S(2)}) collective-permute-start(bf16[1024,128]{1,0:T(8,128)(2,1)S(1)} %fusion.120), channel_id=1, source_target_pairs={{0,32},{32,64},{64,96},{96,128},{128,160},{160,192},{192,224},{1,3... | collective-permute-start | bytes 786440 | tf_op jit(solution)/shard_map/while/body/eval_jaxpr/ppermute | solution.py:29
  371.9 10.7 %collective-permute-start.5 = (bf16[1024,128]{1,0:T(8,128)(2,1)S(1)}, bf16[1024,128]{1,0:T(8,128)(2,1)S(1)}, u32[]{:S(2)}, u32[]{:S(2)}) collective-permute-start(bf16[1024,128]{1,0:T(8,128)(2,1)S(1)} %fusion.120), channel_id=1, source_target_pairs={{0,32},{32,64},{64,96},{96,128},{128,160},{160,192},{192,224},{1,3... | collective-permute-start | bytes 786440 | tf_op jit(solution)/shard_map/while/body/eval_jaxpr/ppermute | solution.py:29
  389.0 10.7 %collective-permute-start.5 = (bf16[1024,128]{1,0:T(8,128)(2,1)S(1)}, bf16[1024,128]{1,0:T(8,128)(2,1)S(1)}, u32[]{:S(2)}, u32[]{:S(2)}) collective-permute-start(bf16[1024,128]{1,0:T(8,128)(2,1)S(1)} %fusion.120), channel_id=1, source_target_pairs={{0,32},{32,64},{64,96},{96,128},{128,160},{160,192},{192,224},{1,3... | collective-permute-start | bytes 786440 | tf_op jit(solution)/shard_map/while/body/eval_jaxpr/ppermute | solution.py:29
  (47 other events, 361.0 us)
where the time goes:
time: 405 us; the launch traced here: 402 us
  waiting for transfers between devices  228 us (56%)
  starting transfers between devices  91.4 us (23%)
  other arithmetic  30.3 us (7%)
  local copies, waits for them, and re-layouts  28 us (7%)
  matrix products  20.6 us (5%)
    ppermute x18, waiting for transfers between devices, passed_along(): return lax.ppermute(value, axis, pairs)  115 us
    ppermute x22, waiting for transfers between devices, extended_2(): before = lax.ppermute(last, axis, up)  86.5 us
    ppermute x18, starting transfers between devices, passed_along(): return lax.ppermute(value, axis, pairs)  66.1 us
    ppermute x22, waiting for transfers between devices, extended_2(): after = lax.ppermute(first, axis, down)  27.2 us
    ppermute x22, starting transfers between devices, extended_2(): after = lax.ppermute(first, axis, down)  20.6 us
    convert_element_type x3, local copies, waits for them, and re-layouts, banded(): return jnp.einsum('isp,iasc->iapc', selector, split_blocks, preferred_ele...  9.89 us
  transfers between devices with their start and end apart: 62, of which 53 were waited for; matrix products, arithmetic and copies ran while one was open for 7% of the time, Pallas kernels for 0%

commit v1 on v0

v1 whole, which is shorter than its diff:
```python
import functools

import jax
import jax.numpy as jnp
from jax import lax
from jax.experimental import pallas as pl
from jax.experimental.pallas import tpu as pltpu
from jax.sharding import PartitionSpec as P

WIN = 8
LEV = 128
SLAB = LEV // WIN
OWN = 1024
BLK = 64
ROWS = OWN // BLK
RU, NNZ_U = 4, 8
RM, NNZ_M = 2, 4
TURN = RM * BLK
HALO = (WIN - 1) * TURN
EXT = OWN + 2 * HALO
END = HALO + OWN
RIM = RU * BLK
M_SIDE = HALO // BLK
M_PAIRS = EXT // 128
FOURS = OWN // 256
EARLY = 3
RELAX = 0.75
MESH = pl.DeviceIdType.MESH
F32 = jnp.float32
BF16 = jnp.bfloat16


def rows_of(window):
    if isinstance(window, int):
        return pl.ds(window * SLAB, SLAB)
    return pl.ds(pl.multiple_of(window * SLAB, SLAB), SLAB)


def lane_index():
    return lax.broadcasted_iota(jnp.int32, (1, 128), 1)


def spread_positions(pattern, first_row, reach, total):
    count = pattern.shape[0]
    own_row = first_row + lax.broadcasted_iota(jnp.int32, (count, ROWS), 1)
    offset = pattern - own_row + reach
    offset = jnp.where(offset < 0, offset + total, offset)
    offset = jnp.where(offset >= total, offset - total, offset)
    offset = jnp.transpose(offset.astype(F32))
    low = lax.broadcasted_iota(jnp.int32, (ROWS, 128), 1) < BLK
    spread = []
    for pair in range(count // 2):
        even = jnp.broadcast_to(offset[:, 2 * pair : 2 * pair + 1], (ROWS, 128))
        odd = jnp.broadcast_to(offset[:, 2 * pair + 1 : 2 * pair + 2], (ROWS, 128))
        spread.append(jnp.where(low, even, odd))
        spread.append(jnp.where(low, odd, even))
    return spread


def place_row(raw, positions, count, first_position):
    terms = []
    for pair in range(raw.shape[1] // 128):
        part = raw[:, pair * 128 : (pair + 1) * 128]
        turned = pltpu.roll(part.astype(F32), BLK, 1).astype(BF16)
        terms.append((part, positions[2 * pair]))
        terms.append((turned, positions[2 * pair + 1]))
    upper = (lane_index() >= BLK).astype(jnp.int32)
    tiles = []
    for v in range(count):
        wanted = (first_position + 2 * v + upper).astype(F32)
        total = None
        for part, position in terms:
            mask = jnp.broadcast_to((position == wanted).astype(F32), (16, 128)).astype(BF16)
            term = part * jnp.concatenate([mask] * (BLK // 16), axis=0)
            total = term if total is None else total + term
        tiles.append(total)
    return tiles


def weights(band, m):
    return jnp.concatenate(
        [band[m - 1 + s, :, 384 - 128 * s : 640 - 128 * s] for s in range(4)], axis=0
    )


def split(value):
    high = value.astype(BF16)
    return high, (value - high.astype(F32)).astype(BF16)


def kernel(
    ncol,
    inc,
    dep,
    og,
    ow,
    es,
    cb,
    cp,
    mb,
    mp,
    x_out,
    d_out,
    inc_v,
    og_v,
    ow_v,
    dep_v,
    es_v,
    g_t,
    dep_t,
    es_t,
    g_f,
    dep_f,
    es_f,
    d_f,
    d_lo,
    s_f,
    p_out,
    p_in,
    i_f,
    t_own,
    t_f,
    x_f,
    x_lo,
    x_r,
    d_r,
    m_raw,
    c_raw,
    m_pat,
    c_pat,
    m_pos,
    c_pos,
    m_band,
    m_turn,
    u_band,
    local_sem,
    g_send,
    g_recv,
    es_send,
    es_recv,
    dep_send,
    dep_recv,
    dr_send,
    dr_recv,
    xr_send,
    xr_recv,
    side_send,
    side_recv,
    gh_send,
    gh_recv,
    p_send,
    p_recv,
    th_send,
    th_recv,
):
    me = lax.axis_index("win")
    col = lax.axis_index("col")
    left = lax.rem(col + ncol - 1, ncol)
    right = lax.rem(col + 1, ncol)
    sides = (left, right)
    total_blocks = ncol * ROWS
    own_cols = pl.ds(HALO, OWN)
    whole = pl.ds(0, OWN)
    every = pl.ds(0, 128)
    sent, due = [], {}

    def to_window(src, dst, send, recv, window):
        return pltpu.make_async_remote_copy(
            src_ref=src, dst_ref=dst, send_sem=send, recv_sem=recv,
            device_id=(window, col), device_id_type=MESH,
        )

    def to_side(src, dst, send, recv, side):
        return pltpu.make_async_remote_copy(
            src_ref=src, dst_ref=dst, send_sem=send, recv_sem=recv,
            device_id=(me, sides[side]), device_id_type=MESH,
        )

    def arrive(*key):
        due.pop(key)()

    def start_sides(key, copies):
        for copy in copies:
            copy.start()
            sent.append(copy.wait_send)
        due[key] = lambda: [copy.wait_recv() for copy in copies]

    def give_out(name, src, dst, cols, sends, recvs):
        for d in range(1, WIN):
            window = lax.rem(me + d, WIN)
            to_window(
                src.at[rows_of(window), :], dst.at[rows_of(me), cols], sends.at[window], recvs.at[me], window
            ).start()
        for k in range(WIN):
            def slab(k=k):
                return to_window(
                    src.at[rows_of(k), :], dst.at[rows_of(k), cols], sends.at[k], recvs.at[k], k
                )

            def sent_slab(slab=slab, k=k):
                @pl.when(me != k)
                def _():
                    slab().wait_send()

            def due_slab(slab=slab, k=k):
                @pl.when(me != k)
                def _():
                    slab().wait_recv()

            sent.append(sent_slab)
            due[name, k] = due_slab

    def give_back(name, src, dst, k, sends, recvs):
        def back():
            return to_window(src.at[rows_of(k), own_cols], dst.at[rows_of(me), :], sends.at[k], recvs.at[me], k)

        @pl.when(me != k)
        def _():
            back().start()

        @pl.when(me == k)
        def _():
            dst[rows_of(me), :] = src[rows_of(k), HALO:END]

        def sent_back():
            @pl.when(me != k)
            def _():
                back().wait_send()

        def due_back():
            @pl.when(me != k)
            def _():
                to_window(dst.at[rows_of(k), :], dst.at[rows_of(k), :], sends.at[k], recvs.at[k], k).wait_recv()

        sent.append(sent_back)
        due[name, k] = due_back

    def halo_copies(src, window, width, sends, recvs):
        rows = rows_of(window)
        return (
            to_side(
                src.at[rows, pl.ds(HALO, width)], src.at[rows, pl.ds(END, width)],
                sends.at[window, 0], recvs.at[window, 0], 0,
            ),
            to_side(
                src.at[rows, pl.ds(END - width, width)], src.at[rows, pl.ds(HALO - width, width)],
                sends.at[window, 1], recvs.at[window, 1], 1,
            ),
        )

    def close():
        for key in list(due):
            arrive(*key)
        for wait in sent:
            wait()

    barrier = pltpu.get_barrier_semaphore()
    for d in range(1, WIN):
        pl.semaphore_signal(barrier, inc=1, device_id=(lax.rem(me + d, WIN), col), device_id_type=MESH)
    for side in range(2):
        pl.semaphore_signal(barrier, inc=1, device_id=(me, sides[side]), device_id_type=MESH)

    loads = [
        pltpu.make_async_copy(inc.at[0], inc_v, local_sem.at[0]),
        pltpu.make_async_copy(og.at[0], og_v, local_sem.at[1]),
        pltpu.make_async_copy(ow.at[0], ow_v, local_sem.at[2]),
        pltpu.make_async_copy(es, es_v, local_sem.at[3]),
        pltpu.make_async_copy(mp, m_pat.at[1], local_sem.at[4]),
        pltpu.make_async_copy(cp, c_pat, local_sem.at[5]),
        pltpu.make_async_copy(mb, m_raw.at[pl.ds(ROWS, ROWS)], local_sem.at[6]),
        pltpu.make_async_copy(cb, c_raw, local_sem.at[7]),
        pltpu.make_async_copy(dep.at[0], dep_v, local_sem.at[8]),
    ]
    for load in loads:
        load.start()
    for load in loads[:4]:
        load.wait()
    for c in range(OWN // 128):
        at = slice(c * 128, (c + 1) * 128)
        g = ow_v[at, :].astype(F32) * inc_v[at, :] - og_v[at, :]
        g_t[:, at] = jnp.transpose(g).astype(BF16)
    es_t[...] = jnp.transpose(jnp.broadcast_to(es_v[...], (128, LEV)))

    pl.semaphore_wait(barrier, WIN + 1)

    give_out("g", g_t, g_f, own_cols, g_send, g_recv)
    n = M_SIDE
    start_sides(
        ("pattern",),
        (
            to_side(mp, m_pat.at[2], side_send.at[0, 0], side_recv.at[0, 0], 0),
            to_side(mp, m_pat.at[0], side_send.at[0, 1], side_recv.at[0, 1], 1),
        ),
    )
    start_sides(
        ("blocks",),
        (
            to_side(mb.at[pl.ds(0, n)], m_raw.at[pl.ds(2 * ROWS, n)], side_send.at[1, 0], side_recv.at[1, 0], 0),
            to_side(mb.at[pl.ds(ROWS - n, n)], m_raw.at[pl.ds(ROWS - n, n)], side_send.at[1, 1], side_recv.at[1, 1], 1),
        ),
    )
    give_out("es", es_t, es_f, every, es_send, es_recv)
    g_f[rows_of(me), HALO:END] = g_t[rows_of(me), :]
    es_f[rows_of(me), :] = es_t[rows_of(me), :]

    def store_positions(side):
        where = slice(side * ROWS, (side + 1) * ROWS)
        block = (left, col, right)[side] * ROWS
        for n, value in enumerate(spread_positions(m_pat[side], block, RM, total_blocks)):
            m_pos[n, where, :] = value

    def build_m(first, last):
        def pair(q, carry):
            zero = jnp.zeros((128, 128), BF16)
            m_band[q, :, 0:128] = zero
            m_band[q, :, 512:640] = zero
            for half in range(2):
                row = 2 * q + (ROWS - M_SIDE) + half
                positions = [m_pos[n, pl.ds(row, 1), :] for n in range(NNZ_M)]
                tiles = place_row(m_raw[row], positions, 3, -half)
                for v, tile in enumerate(tiles):
                    m_band[q, half * BLK : (half + 1) * BLK, (v + 1) * 128 : (v + 2) * 128] = tile
            return carry

        lax.fori_loop(first, last, pair, 0)

    def build_u():
        def four(r, carry):
            zero = jnp.zeros((BLK, 128), BF16)
            for sub in range(4):
                row = 4 * r + sub
                where = slice(sub * BLK, (sub + 1) * BLK)
                positions = [c_pos[n, pl.ds(row, 1), :] for n in range(NNZ_U)]
                start = sub // 2
                tiles = place_row(c_raw[row], positions, 5, 2 * start - sub)
                for v, tile in enumerate(tiles):
                    u_band[r, where, (v + start) * 128 : (v + start + 1) * 128] = tile
                u_band[r, where, 5 * (1 - start) * 128 : (5 * (1 - start) + 1) * 128] = zero
            return carry

        lax.fori_loop(0, FOURS, four, 0)

    def turn_tile(p, q_shift):
        tile = m_band[p + q_shift, :, 256 - 128 * q_shift : 384 - 128 * q_shift]
        at = 256 + 128 * q_shift
        m_turn[p, :, at : at + 128] = jnp.transpose(tile)

    def build_turn():
        zero = jnp.zeros((128, 128), BF16)

        def one(p, carry):
            m_turn[p, :, 0:128] = zero
            m_turn[p, :, 512:640] = zero
            for q_shift in (-1, 0, 1):
                turn_tile(p, q_shift)
            return carry

        lax.fori_loop(1, M_PAIRS - 1, one, 0)
        for p, shifts in ((0, (0, 1)), (M_PAIRS - 1, (-1, 0))):
            for v in range(5):
                m_turn[p, :, v * 128 : (v + 1) * 128] = zero
            for q_shift in shifts:
                turn_tile(p, q_shift)

    for load in loads[4:8]:
        load.wait()
    store_positions(1)
    for n, value in enumerate(spread_positions(c_pat[...], col * ROWS, RU, total_blocks)):
        c_pos[n] = value
    side_pairs = M_SIDE // 2
    build_m(side_pairs, side_pairs + ROWS // 2)
    build_u()
    loads[8].wait()
    for c in range(OWN // 128):
        at = slice(c * 128, (c + 1) * 128)
        dep_t[:, at] = jnp.transpose(dep_v[at, :]).astype(BF16)
    for k in range(WIN - 1, -1, -1):
        arrive("g", k)
        if k:
            start_sides(("g halo", k), halo_copies(g_f, k, TURN * k, gh_send, gh_recv))
    give_out("dep", dep_t, dep_f, whole, dep_send, dep_recv)
    dep_f[rows_of(me), :] = dep_t[rows_of(me), :]
    arrive("pattern")
    store_positions(0)
    store_positions(2)
    arrive("blocks")
    build_m(0, side_pairs)
    build_m(side_pairs + ROWS // 2, M_PAIRS)
    for k in range(WIN):
        arrive("es", k)

    def scaled(k):
        scale = jnp.concatenate([es_f[rows_of(k), :]] * 2, axis=1)
        return lambda value: (scale * value).astype(BF16)

    def transposed(rows, c):
        total = None
        for r in range(max(c - 1, 0), min(c + 2, FOURS)):
            at = (c - r + 1) * 256
            term = jnp.dot(
                s_f[rows, r * 256 : (r + 1) * 256], u_band[r, :, at : at + 256], preferred_element_type=F32
            )
            total = term if total is None else total + term
        return total

    def send_rims(part, rows):
        for side, groups in ((0, (-1, 0)), (1, (FOURS - 1, FOURS))):
            for n, c in enumerate(groups):
                p_out[side, rows, n * 256 : (n + 1) * 256] = transposed(rows, c).astype(BF16)
        start_sides(
            ("rims", part),
            tuple(
                to_side(p_out.at[side, rows, :], p_in.at[1 - side, rows, :], p_send.at[part, side], p_recv.at[part, side], side)
                for side in range(2)
            ),
        )

    last = WIN - 1
    arrive("g halo", last)
    d_f[rows_of(last), :] = g_f[rows_of(last), :]
    give_back("d", d_f, d_r, last, dr_send, dr_recv)
    scale = scaled(last)
    for r in range(FOURS):
        s_f[rows_of(last), r * 256 : (r + 1) * 256] = scale(
            g_f[rows_of(last), HALO + r * 256 : HALO + (r + 1) * 256].astype(F32)
        )
    for k in range(last - 1, -1, -1):
        if k:
            arrive("g halo", k)
        scale = jnp.concatenate([es_f[rows_of(k), :]] * 2, axis=1)
        for group in range(OWN // 256 + k):
            m = M_SIDE // 2 - k + 2 * group
            at = slice(m * 128, (m + 2) * 128)
            near = slice((m - 1) * 128, (m + 3) * 128)
            field = d_f[rows_of(k + 1), near]
            if k + 1 < last:
                field = jnp.concatenate([field, d_lo[rows_of(k + 1), near]], axis=0)
            product = jnp.dot(field, weights(m_band, m), preferred_element_type=F32)
            if k + 1 < last:
                product = product[:SLAB] + product[SLAB:]
            value = g_f[rows_of(k), at].astype(F32) + product
            d_f[rows_of(k), at], d_lo[rows_of(k), at] = split(value)
            value = (scale * value).astype(BF16)
            for n in range(2):
                c = m + n - M_SIDE // 2
                if 0 <= c < OWN // 128:
                    s_f[rows_of(k), c * 128 : (c + 1) * 128] = value[:, n * 128 : (n + 1) * 128]
        give_back("d", d_f, d_r, k, dr_send, dr_recv)
        if k == EARLY:
            send_rims(0, slice(EARLY * SLAB, LEV))
    send_rims(1, slice(0, EARLY * SLAB))

    every_row = slice(0, LEV)
    inner = {c: transposed(every_row, c) for c in range(1, FOURS - 1)}
    for c in inner:
        i_f[:, (c + 1) * 256 : (c + 2) * 256] = inner[c].astype(BF16)
    build_turn()
    for k in range(WIN):
        arrive("dep", k)
    arrive("rims", 0)
    arrive("rims", 1)
    for side, groups in ((0, (-1, 0)), (1, (FOURS - 1, FOURS))):
        for n, c in enumerate(groups):
            there = p_in[side, :, n * 256 : (n + 1) * 256].astype(F32)
            i_f[:, (c + 1) * 256 : (c + 2) * 256] = (transposed(every_row, c) + there).astype(BF16)
    scale = es_f[...]
    scale = jnp.concatenate([scale, scale], axis=1)
    for r in range(FOURS):
        product = lax.dot_general(
            i_f[:, r * 256 : r * 256 + 768], u_band[r], (((1,), (1,)), ((), ())), preferred_element_type=F32
        )
        at = slice(r * 256, (r + 1) * 256)
        value = dep_f[:, at].astype(F32) - scale * product
        t_own[:, at] = value
        t_f[:, HALO + r * 256 : HALO + (r + 1) * 256] = value.astype(BF16)

    for k in range(WIN - 1):
        start_sides(("t halo", k), halo_copies(t_f, k, HALO - TURN * k, th_send, th_recv))

    def target(k, m):
        c = m - M_SIDE // 2
        if 0 <= c < OWN // 128:
            return t_own[rows_of(k), c * 128 : (c + 1) * 128]
        return t_f[rows_of(k), m * 128 : (m + 1) * 128].astype(F32)

    for c in range(OWN // 128):
        at = slice(HALO + c * 128, HALO + (c + 1) * 128)
        x_f[rows_of(0), at], x_lo[rows_of(0), at] = split(t_own[rows_of(0), c * 128 : (c + 1) * 128])
    give_back("x", x_f, x_r, 0, xr_send, xr_recv)
    arrive("t halo", 0)
    for at in (slice(0, HALO), slice(END, EXT)):
        x_f[rows_of(0), at] = t_f[rows_of(0), at]
        x_lo[rows_of(0), at] = jnp.zeros((SLAB, HALO), BF16)
    for k in range(1, WIN):
        if k < WIN - 1:
            arrive("t halo", k)
        for group in range(OWN // 256 + WIN - 1 - k):
            m = k + 2 * group
            at = slice(m * 128, (m + 2) * 128)
            near = slice((m - 1) * 128, (m + 3) * 128)
            field = jnp.concatenate([x_f[rows_of(k - 1), near], x_lo[rows_of(k - 1), near]], axis=0)
            product = jnp.dot(field, weights(m_turn, m), preferred_element_type=F32)
            base = jnp.concatenate([target(k, m), target(k, m + 1)], axis=1)
            x_f[rows_of(k), at], x_lo[rows_of(k), at] = split(base + product[:SLAB] + product[SLAB:])
        give_back("x", x_f, x_r, k, xr_send, xr_recv)

    def finish(name, result, out):
        for k in range(WIN):
            arrive(name, k)
        for c in range(OWN // 128):
            at = slice(c * 128, (c + 1) * 128)
            out[at, :] = jnp.transpose(result[:, at].astype(F32)).astype(BF16)

    finish("d", d_r, d_out)
    finish("x", x_r, x_out)
    close()


def body(
    increment,
    dual_field,
    departure,
    obs_grad,
    obs_weight,
    error_scale,
    corr_blocks,
    corr_pattern,
    model_blocks,
    model_pattern,
):
    ncol = lax.axis_size("col")
    vmem = pltpu.VMEM
    dma = pltpu.SemaphoreType.DMA
    hbm = pl.BlockSpec(memory_space=pltpu.HBM)
    x_new, d_new = pl.pallas_call(
        functools.partial(kernel, ncol),
        out_shape=[jax.ShapeDtypeStruct((OWN, LEV), BF16)] * 2,
        in_specs=[hbm] * 9,
        out_specs=[pl.BlockSpec(memory_space=pltpu.VMEM)] * 2,
        scratch_shapes=[
            vmem((OWN, LEV), F32),
            vmem((OWN, LEV), F32),
            vmem((OWN, LEV), BF16),
            vmem((OWN, LEV), F32),
            vmem((1, LEV), F32),
            vmem((LEV, OWN), BF16),
            vmem((LEV, OWN), BF16),
            vmem((LEV, 128), F32),
            vmem((LEV, EXT), BF16),
            vmem((LEV, OWN), BF16),
            vmem((LEV, 128), F32),
            vmem((LEV, EXT), BF16),
            vmem((LEV, EXT), BF16),
            vmem((LEV, OWN), BF16),
            vmem((2, LEV, 2 * RIM), BF16),
            vmem((2, LEV, 2 * RIM), BF16),
            vmem((LEV, OWN + 2 * RIM), BF16),
            vmem((LEV, OWN), F32),
            vmem((LEV, EXT), BF16),
            vmem((LEV, EXT), BF16),
            vmem((LEV, EXT), BF16),
            vmem((LEV, OWN), BF16),
            vmem((LEV, OWN), BF16),
            vmem((3 * ROWS, BLK, NNZ_M * BLK), BF16),
            vmem((ROWS, BLK, NNZ_U * BLK), BF16),
            vmem((3, NNZ_M, ROWS), jnp.int32),
            vmem((NNZ_U, ROWS), jnp.int32),
            vmem((NNZ_M, 3 * ROWS, 128), F32),
            vmem((NNZ_U, ROWS, 128), F32),
            vmem((M_PAIRS, 128, 640), BF16),
            vmem((M_PAIRS, 128, 640), BF16),
            vmem((FOURS, 256, 768), BF16),
            dma((9,)),
        ]
        + [dma((WIN,))] * 10
        + [dma((2, 2))] * 2
        + [dma((WIN, 2))] * 2
        + [dma((2, 2))] * 2
        + [dma((WIN, 2))] * 2,
        compiler_params=pltpu.CompilerParams(
            collective_id=0, has_side_effects=True, vmem_limit_bytes=56 * 1024 * 1024
        ),
    )(
        increment,
        departure,
        obs_grad,
        obs_weight,
        error_scale,
        corr_blocks,
        corr_pattern.T,
        model_blocks,
        model_pattern.T,
    )
    increment_next = (1.0 - RELAX) * increment + RELAX * x_new.astype(F32)[None]
    dual_next = (1.0 - RELAX) * dual_field + RELAX * d_new.astype(F32)[None]
    return increment_next, dual_next


def solution(mesh):
    field = P("win", "col", None)
    return jax.shard_map(
        body,
        mesh=mesh,
        in_specs=(
            field,
            field,
            field,
            field,
            field,
            P("win", None),
            P("col", None, None),
            P("col", None),
            P("col", None, None),
            P("col", None),
        ),
        out_specs=(field, field),
        check_vma=False,
    )
```

time: 405 us -> 47.8 us (0.12)
  waiting for transfers between devices: 228 us -> 0 us
  starting transfers between devices: 91.4 us -> 0 us
  Pallas kernels: 0 us -> 44.7 us
  other arithmetic: 30.3 us -> 2.13 us
  local copies, waits for them, and re-layouts: 28 us -> 0.01 us
  matrix products: 20.6 us -> 0 us
    ppermute x62 -> x0, waiting for transfers between devices: 228 us -> none  [the longest x18 115 us: passed_along(): return lax.ppermute(value, axis, pairs)]
    ppermute x62 -> x0, starting transfers between devices: 91.4 us -> none  [the longest x18 66.1 us: passed_along(): return lax.ppermute(value, axis, pairs)]
    pallas_call x0 -> x1, Pallas kernels: none -> 44.7 us  [body(): pl.pallas_call(functools.partial(kernel, ncol), out_shape=[jax.ShapeDtype...]
    dot_general x14 -> x0, matrix products: 13.6 us -> none  [the longest x2 7.21 us: banded(): jnp.einsum('isp,iasc->iapc', selector, split_blocks, preferred_element_ty...]
    convert_element_type x3 -> x0, local copies, waits for them, and re-layouts: 9.89 us -> none  [banded(): return jnp.einsum('isp,iasc->iapc', selector, split_blocks, preferred_ele...]
    add x11 -> x1, other arithmetic: 10.8 us -> 2.13 us  [body(): dual_next = (1.0 - RELAX) * dual_field + RELAX * d_new.astype(F32)[None]]
    another operation x8 -> x0, other arithmetic: 7.56 us -> none  [back_turn(): held_states = jnp.stack(fresh_states)]
    scatter-add x63 -> x0, other arithmetic: 6.05 us -> none  [the longest x52 5.29 us: band_spread(): spread_sum = spread_sum.at[:, slot_index * block_width:slot_index * block...]
  transfers between devices with their start and end apart: 62 -> 0, of which waited for: 53 -> 0; matrix products, arithmetic and copies ran while one was open for 7% -> 0% of each run, Pallas kernels for 0% -> 0%
where the time goes in v1:
time: 47.8 us; the launch traced here: 47.5 us
  Pallas kernels  44.7 us (94%)
  other arithmetic  2.13 us (4%)
  between operations  0.67 us (1%)
    pallas_call x1, Pallas kernels, body(): pl.pallas_call(functools.partial(kernel, ncol), out_shape=[jax.ShapeDtype...  44.7 us
    add x1, other arithmetic, body(): dual_next = (1.0 - RELAX) * dual_field + RELAX * d_new.astype(F32)[None]  2.13 us

profile of v1, /device:TPU:6, one launch (start us, length us, event | category | flops | bytes accessed | tf_op | source)
XLA Modules:
  0.0 47.5 jit_solution(1352112081496868001)
XLA Ops:
  0.6 0.0 copy-start
  0.6 0.0 copy-start.1
  0.7 44.7 %shard_map.113 = (bf16[1024,128]{1,0:T(8,128)(2,1)}, bf16[1024,128]{1,0:T(8,128)(2,1)}) custom-call(f32[1,1024,128]{2,1,0:T(8,128)} %inc.1, f32[1,1024,128]{2,1,0:T(8,128)} %dep.1, f32[1,1024,128]{2,1,0:T(8,128)} %og.1, bf16[1,1024,128]{2,1,0:T(8,128)(2,1)} %ow.1, f32[1,128]{1,0:T(1,128)} %es.1, bf16[16,64,512]{2,1,0:T(8,128)(2,1)} %cb.1, s32[8,16]{1,0:T(8,128)} %bitcast.6, ...), custom_call_target="tpu_custom_call" | custom-call | tf_op jit(solution)/shard_map/pallas_call | solution.py:535
  45.4 0.0 copy-done
  45.4 0.0 copy-done.1
  45.4 2.1 %bitcast_add_fusion = (f32[1,1024,128]{2,1,0:T(8,128)}, f32[1,1024,128]{2,1,0:T(8,128)}) fusion(bf16[1024,128]{1,0:T(8,128)(2,1)} %get-tuple-element.5, f32[1,1024,128]{2,1,0:T(8,128)S(1)} %copy-done.1, bf16[1024,128]{1,0:T(8,128)(2,1)} %get-tuple-element.4, f32[1,1024,128]{2,1,0:T(8,128)S(1)} %copy-done), kind=kLoop, calls=%fused_computation | loop fusion | flops 1048576 | bytes 2621440 | tf_op jit(solution)/shard_map/add | solution.py:595
Async XLA Ops:
  0.6 44.8 %copy-start = (f32[1,1024,128]{2,1,0:T(8,128)S(1)}, f32[1,1024,128]{2,1,0:T(8,128)}, u32[]{:S(2)}) copy-start(f32[1,1024,128]{2,1,0:T(8,128)} %inc.1) | copy-start | bytes 1572868
  0.6 44.8 %copy-start.1 = (f32[1,1024,128]{2,1,0:T(8,128)S(1)}, f32[1,1024,128]{2,1,0:T(8,128)}, u32[]{:S(2)}) copy-start(f32[1,1024,128]{2,1,0:T(8,128)} %param.11) | copy-start | bytes 1572868

commit v2 on v1

--- a/solution.py
+++ b/solution.py
@@ -158,6 +158,7 @@
     left = lax.rem(col + ncol - 1, ncol)
     right = lax.rem(col + 1, ncol)
     sides = (left, right)
+    partner = me + 1 - 2 * lax.rem(me, 2)
     total_blocks = ncol * ROWS
     own_cols = pl.ds(HALO, OWN)
     whole = pl.ds(0, OWN)
@@ -170,10 +171,10 @@
             device_id=(window, col), device_id_type=MESH,
         )
 
-    def to_side(src, dst, send, recv, side):
+    def to_side(src, dst, send, recv, side, window=me):
         return pltpu.make_async_remote_copy(
             src_ref=src, dst_ref=dst, send_sem=send, recv_sem=recv,
-            device_id=(me, sides[side]), device_id_type=MESH,
+            device_id=(window, sides[side]), device_id_type=MESH,
         )
 
     def arrive(*key):
@@ -227,13 +228,16 @@
             def _():
                 back().wait_send()
 
-        def due_back():
-            @pl.when(me != k)
+        sent.append(sent_back)
+
+    def due_back(name, dst, sends, recvs, here):
+        def back(k):
+            @pl.when((me != k) & here)
             def _():
                 to_window(dst.at[rows_of(k), :], dst.at[rows_of(k), :], sends.at[k], recvs.at[k], k).wait_recv()
 
-        sent.append(sent_back)
-        due[name, k] = due_back
+        for k in range(WIN):
+            due[name, k] = lambda k=k: back(k)
 
     def halo_copies(src, window, width, sends, recvs):
         rows = rows_of(window)
@@ -257,8 +261,9 @@
     barrier = pltpu.get_barrier_semaphore()
     for d in range(1, WIN):
         pl.semaphore_signal(barrier, inc=1, device_id=(lax.rem(me + d, WIN), col), device_id_type=MESH)
-    for side in range(2):
-        pl.semaphore_signal(barrier, inc=1, device_id=(me, sides[side]), device_id_type=MESH)
+    for window in (me, partner):
+        for side in range(2):
+            pl.semaphore_signal(barrier, inc=1, device_id=(window, sides[side]), device_id_type=MESH)
 
     loads = [
         pltpu.make_async_copy(inc.at[0], inc_v, local_sem.at[0]),
@@ -281,10 +286,9 @@
         g_t[:, at] = jnp.transpose(g).astype(BF16)
     es_t[...] = jnp.transpose(jnp.broadcast_to(es_v[...], (128, LEV)))
 
-    pl.semaphore_wait(barrier, WIN + 1)
+    pl.semaphore_wait(barrier, WIN - 1 + 4)
 
     give_out("g", g_t, g_f, own_cols, g_send, g_recv)
-    n = M_SIDE
     start_sides(
         ("pattern",),
         (
@@ -292,16 +296,30 @@
             to_side(mp, m_pat.at[0], side_send.at[0, 1], side_recv.at[0, 1], 1),
         ),
     )
-    start_sides(
-        ("blocks",),
-        (
-            to_side(mb.at[pl.ds(0, n)], m_raw.at[pl.ds(2 * ROWS, n)], side_send.at[1, 0], side_recv.at[1, 0], 0),
-            to_side(mb.at[pl.ds(ROWS - n, n)], m_raw.at[pl.ds(ROWS - n, n)], side_send.at[1, 1], side_recv.at[1, 1], 1),
-        ),
-    )
+    half = M_SIDE // 2
+    across = (lax.rem(col, ncol // 2) == 0, lax.rem(col + 1, ncol // 2) == 0)
+    for part in range(2):
+        copies = []
+        for side, first in ((0, part * half), (1, ROWS - M_SIDE + part * half)):
+            rows = (pl.ds(2 * ROWS + first, half), pl.ds(first, half))[side]
+            window = jnp.where(across[side], partner, me) if part else me
+            copies.append(
+                to_side(
+                    mb.at[pl.ds(first, half)], m_raw.at[rows],
+                    side_send.at[1 + part, side], side_recv.at[1 + part, side], side, window,
+                )
+            )
+        start_sides(("blocks", part), tuple(copies))
     give_out("es", es_t, es_f, every, es_send, es_recv)
     g_f[rows_of(me), HALO:END] = g_t[rows_of(me), :]
     es_f[rows_of(me), :] = es_t[rows_of(me), :]
+
+    loads[8].wait()
+    for c in range(OWN // 128):
+        at = slice(c * 128, (c + 1) * 128)
+        dep_t[:, at] = jnp.transpose(dep_v[at, :]).astype(BF16)
+    give_out("dep", dep_t, dep_f, whole, dep_send, dep_recv)
+    dep_f[rows_of(me), :] = dep_t[rows_of(me), :]
 
     def store_positions(side):
         where = slice(side * ROWS, (side + 1) * ROWS)
@@ -370,20 +388,15 @@
     side_pairs = M_SIDE // 2
     build_m(side_pairs, side_pairs + ROWS // 2)
     build_u()
-    loads[8].wait()
-    for c in range(OWN // 128):
-        at = slice(c * 128, (c + 1) * 128)
-        dep_t[:, at] = jnp.transpose(dep_v[at, :]).astype(BF16)
     for k in range(WIN - 1, -1, -1):
         arrive("g", k)
         if k:
             start_sides(("g halo", k), halo_copies(g_f, k, TURN * k, gh_send, gh_recv))
-    give_out("dep", dep_t, dep_f, whole, dep_send, dep_recv)
-    dep_f[rows_of(me), :] = dep_t[rows_of(me), :]
     arrive("pattern")
     store_positions(0)
     store_positions(2)
-    arrive("blocks")
+    arrive("blocks", 0)
+    arrive("blocks", 1)
     build_m(0, side_pairs)
     build_m(side_pairs + ROWS // 2, M_PAIRS)
     for k in range(WIN):
@@ -418,7 +431,6 @@
     last = WIN - 1
     arrive("g halo", last)
     d_f[rows_of(last), :] = g_f[rows_of(last), :]
-    give_back("d", d_f, d_r, last, dr_send, dr_recv)
     scale = scaled(last)
     for r in range(FOURS):
         s_f[rows_of(last), r * 256 : (r + 1) * 256] = scale(
@@ -445,10 +457,12 @@
                 c = m + n - M_SIDE // 2
                 if 0 <= c < OWN // 128:
                     s_f[rows_of(k), c * 128 : (c + 1) * 128] = value[:, n * 128 : (n + 1) * 128]
-        give_back("d", d_f, d_r, k, dr_send, dr_recv)
         if k == EARLY:
             send_rims(0, slice(EARLY * SLAB, LEV))
     send_rims(1, slice(0, EARLY * SLAB))
+    for k in range(last):
+        give_back("d", d_f, d_r, k, dr_send, dr_recv)
+    due_back("d", d_r, dr_send, dr_recv, me != last)
 
     every_row = slice(0, LEV)
     inner = {c: transposed(every_row, c) for c in range(1, FOURS - 1)}
@@ -503,6 +517,7 @@
             base = jnp.concatenate([target(k, m), target(k, m + 1)], axis=1)
             x_f[rows_of(k), at], x_lo[rows_of(k), at] = split(base + product[:SLAB] + product[SLAB:])
         give_back("x", x_f, x_r, k, xr_send, xr_recv)
+    due_back("x", x_r, xr_send, xr_recv, me >= 0)
 
     def finish(name, result, out):
         for k in range(WIN):
@@ -510,6 +525,10 @@
         for c in range(OWN // 128):
             at = slice(c * 128, (c + 1) * 128)
             out[at, :] = jnp.transpose(result[:, at].astype(F32)).astype(BF16)
+
+    @pl.when(me == last)
+    def _():
+        d_r[...] = g_t[...]
 
     finish("d", d_r, d_out)
     finish("x", x_r, x_out)
@@ -534,7 +553,7 @@
     hbm = pl.BlockSpec(memory_space=pltpu.HBM)
     x_new, d_new = pl.pallas_call(
         functools.partial(kernel, ncol),
-        out_shape=[jax.ShapeDtypeStruct((OWN, LEV), BF16)] * 2,
+        out_shape=[pltpu.VMEM((OWN, LEV), BF16)] * 2,
         in_specs=[hbm] * 9,
         out_specs=[pl.BlockSpec(memory_space=pltpu.VMEM)] * 2,
         scratch_shapes=[
@@ -573,7 +592,7 @@
             dma((9,)),
         ]
         + [dma((WIN,))] * 10
-        + [dma((2, 2))] * 2
+        + [dma((3, 2))] * 2
         + [dma((WIN, 2))] * 2
         + [dma((2, 2))] * 2
         + [dma((WIN, 2))] * 2,

time: 47.8 us -> 44.5 us (0.931)
  Pallas kernels: 44.7 us -> 42.6 us
  other arithmetic: 2.13 us -> 1.1 us
    pallas_call x1, Pallas kernels: 44.7 us -> 42.6 us  [body(): pl.pallas_call(functools.partial(kernel, ncol), out_shape=[pltpu.VMEM((OW...]
    add x1, other arithmetic: 2.13 us -> 1.1 us  [body(): dual_next = (1.0 - RELAX) * dual_field + RELAX * d_new.astype(F32)[None]]
where the time goes in v2:
time: 44.5 us; the launch traced here: 44.4 us
  Pallas kernels  42.6 us (96%)
  other arithmetic  1.1 us (2%)
  between operations  0.67 us (2%)
    pallas_call x1, Pallas kernels, body(): pl.pallas_call(functools.partial(kernel, ncol), out_shape=[pltpu.VMEM((OW...  42.6 us
    add x1, other arithmetic, body(): dual_next = (1.0 - RELAX) * dual_field + RELAX * d_new.astype(F32)[None]  1.1 us

profile of v2, /device:TPU:6, one launch (start us, length us, event | category | flops | bytes accessed | tf_op | source)
XLA Modules:
  0.0 44.4 jit_solution(14383291382131967542)
XLA Ops:
  0.6 0.0 copy-start
  0.6 0.0 copy-start.1
  0.7 42.6 %shard_map.113 = (bf16[1024,128]{1,0:T(8,128)(2,1)S(1)}, bf16[1024,128]{1,0:T(8,128)(2,1)S(1)}) custom-call(f32[1,1024,128]{2,1,0:T(8,128)} %inc.1, f32[1,1024,128]{2,1,0:T(8,128)} %dep.1, f32[1,1024,128]{2,1,0:T(8,128)} %og.1, bf16[1,1024,128]{2,1,0:T(8,128)(2,1)} %ow.1, f32[1,128]{1,0:T(1,128)} %es.1, bf16[16,64,512]{2,1,0:T(8,128)(2,1)} %cb.1, ...), custom_call_target="tpu_custom_call" | custom-call | tf_op jit(solution)/shard_map/pallas_call | solution.py:554
  43.3 0.0 copy-done
  43.3 0.0 copy-done.1
  43.3 1.1 %bitcast_add_fusion = (f32[1,1024,128]{2,1,0:T(8,128)}, f32[1,1024,128]{2,1,0:T(8,128)}) fusion(bf16[1024,128]{1,0:T(8,128)(2,1)S(1)} %get-tuple-element.5, f32[1,1024,128]{2,1,0:T(8,128)S(1)} %copy-done.1, bf16[1024,128]{1,0:T(8,128)(2,1)S(1)} %get-tuple-element.4, f32[1,1024,128]{2,1,0:T(8,128)S(1)} %copy-done), kind=kLoop, calls=%fused_computation | loop fusion | flops 1048576 | bytes 2621440 | tf_op jit(solution)/shard_map/add | solution.py:614
Async XLA Ops:
  0.6 42.6 %copy-start = (f32[1,1024,128]{2,1,0:T(8,128)S(1)}, f32[1,1024,128]{2,1,0:T(8,128)}, u32[]{:S(2)}) copy-start(f32[1,1024,128]{2,1,0:T(8,128)} %inc.1) | copy-start | bytes 1572868
  0.6 42.6 %copy-start.1 = (f32[1,1024,128]{2,1,0:T(8,128)S(1)}, f32[1,1024,128]{2,1,0:T(8,128)}, u32[]{:S(2)}) copy-start(f32[1,1024,128]{2,1,0:T(8,128)} %param.11) | copy-start | bytes 1572868

commit v3 on v2

--- a/solution.py
+++ b/solution.py
@@ -23,7 +23,10 @@
 M_SIDE = HALO // BLK
 M_PAIRS = EXT // 128
 FOURS = OWN // 256
-EARLY = 3
+EDGES = (-1, 0, FOURS - 1, FOURS)
+EARLY = 4
+G_GROUPS = ((6, 7), (3, 4, 5), (1, 2))
+T_GROUPS = ((0, 1), (2, 3), (4, 5, 6))
 RELAX = 0.75
 MESH = pl.DeviceIdType.MESH
 F32 = jnp.float32
@@ -111,12 +114,14 @@
     es_t,
     g_f,
     dep_f,
+    es_all,
     es_f,
     d_f,
     d_lo,
     s_f,
     p_out,
     p_in,
+    p_own,
     i_f,
     t_own,
     t_f,
@@ -162,7 +167,6 @@
     total_blocks = ncol * ROWS
     own_cols = pl.ds(HALO, OWN)
     whole = pl.ds(0, OWN)
-    every = pl.ds(0, 128)
     sent, due = [], {}
 
     def to_window(src, dst, send, recv, window):
@@ -187,7 +191,7 @@
         due[key] = lambda: [copy.wait_recv() for copy in copies]
 
     def give_out(name, src, dst, cols, sends, recvs):
-        for d in range(1, WIN):
+        for d in (3, 5, 1, 7, 4, 2, 6):
             window = lax.rem(me + d, WIN)
             to_window(
                 src.at[rows_of(window), :], dst.at[rows_of(me), cols], sends.at[window], recvs.at[me], window
@@ -239,8 +243,9 @@
         for k in range(WIN):
             due[name, k] = lambda k=k: back(k)
 
-    def halo_copies(src, window, width, sends, recvs):
-        rows = rows_of(window)
+    def halo_copies(src, windows, width, sends, recvs):
+        window = windows[0]
+        rows = pl.ds(window * SLAB, len(windows) * SLAB)
         return (
             to_side(
                 src.at[rows, pl.ds(HALO, width)], src.at[rows, pl.ds(END, width)],
@@ -284,7 +289,6 @@
         at = slice(c * 128, (c + 1) * 128)
         g = ow_v[at, :].astype(F32) * inc_v[at, :] - og_v[at, :]
         g_t[:, at] = jnp.transpose(g).astype(BF16)
-    es_t[...] = jnp.transpose(jnp.broadcast_to(es_v[...], (128, LEV)))
 
     pl.semaphore_wait(barrier, WIN - 1 + 4)
 
@@ -310,16 +314,32 @@
                 )
             )
         start_sides(("blocks", part), tuple(copies))
-    give_out("es", es_t, es_f, every, es_send, es_recv)
+    for d in range(1, WIN):
+        window = lax.rem(me + d, WIN)
+        to_window(es_v, es_all.at[me], es_send.at[window], es_recv.at[me], window).start()
+    for k in range(WIN):
+        def scale_row(k=k):
+            return to_window(es_v, es_all.at[k], es_send.at[k], es_recv.at[k], k)
+
+        def sent_row(row=scale_row, k=k):
+            @pl.when(me != k)
+            def _():
+                row().wait_send()
+
+        def due_row(row=scale_row, k=k):
+            @pl.when(me != k)
+            def _():
+                row().wait_recv()
+
+        sent.append(sent_row)
+        due["es", k] = due_row
+    es_all[me] = es_v[...]
     g_f[rows_of(me), HALO:END] = g_t[rows_of(me), :]
-    es_f[rows_of(me), :] = es_t[rows_of(me), :]
 
     loads[8].wait()
     for c in range(OWN // 128):
         at = slice(c * 128, (c + 1) * 128)
         dep_t[:, at] = jnp.transpose(dep_v[at, :]).astype(BF16)
-    give_out("dep", dep_t, dep_f, whole, dep_send, dep_recv)
-    dep_f[rows_of(me), :] = dep_t[rows_of(me), :]
 
     def store_positions(side):
         where = slice(side * ROWS, (side + 1) * ROWS)
@@ -390,8 +410,16 @@
     build_u()
     for k in range(WIN - 1, -1, -1):
         arrive("g", k)
-        if k:
-            start_sides(("g halo", k), halo_copies(g_f, k, TURN * k, gh_send, gh_recv))
+        for windows in G_GROUPS:
+            if k == windows[0]:
+                start_sides(("g halo", windows[-1]), halo_copies(g_f, windows, TURN * windows[-1], gh_send, gh_recv))
+    for k in range(WIN):
+        arrive("es", k)
+    rows = jnp.concatenate([es_all[k] for k in range(WIN)] + [jnp.zeros((128 - WIN, LEV), F32)], axis=0)
+    es_t[...] = jnp.transpose(rows)
+    columns = es_t[rows_of(me), :]
+    for k in range(WIN):
+        es_f[rows_of(k), :] = jnp.broadcast_to(columns[:, k : k + 1], (SLAB, 128))
     arrive("pattern")
     store_positions(0)
     store_positions(2)
@@ -399,9 +427,9 @@
     arrive("blocks", 1)
     build_m(0, side_pairs)
     build_m(side_pairs + ROWS // 2, M_PAIRS)
-    for k in range(WIN):
-        arrive("es", k)
-
+
+    give_out("dep", dep_t, dep_f, whole, dep_send, dep_recv)
+    dep_f[rows_of(me), :] = dep_t[rows_of(me), :]
     def scaled(k):
         scale = jnp.concatenate([es_f[rows_of(k), :]] * 2, axis=1)
         return lambda value: (scale * value).astype(BF16)
@@ -417,16 +445,16 @@
         return total
 
     def send_rims(part, rows):
-        for side, groups in ((0, (-1, 0)), (1, (FOURS - 1, FOURS))):
-            for n, c in enumerate(groups):
-                p_out[side, rows, n * 256 : (n + 1) * 256] = transposed(rows, c).astype(BF16)
-        start_sides(
-            ("rims", part),
-            tuple(
-                to_side(p_out.at[side, rows, :], p_in.at[1 - side, rows, :], p_send.at[part, side], p_recv.at[part, side], side)
-                for side in range(2)
-            ),
+        copies = tuple(
+            to_side(p_out.at[side, rows, :], p_in.at[1 - side, rows, :], p_send.at[part, side], p_recv.at[part, side], side)
+            for side in range(2)
         )
+        for side in range(2):
+            for n in range(2):
+                p_out[side, rows, n * 256 : (n + 1) * 256] = transposed(rows, EDGES[2 * side + n]).astype(BF16)
+            copies[side].start()
+            sent.append(copies[side].wait_send)
+        due["rims", part] = lambda: [copy.wait_recv() for copy in copies]
 
     last = WIN - 1
     arrive("g halo", last)
@@ -437,7 +465,7 @@
             g_f[rows_of(last), HALO + r * 256 : HALO + (r + 1) * 256].astype(F32)
         )
     for k in range(last - 1, -1, -1):
-        if k:
+        if ("g halo", k) in due:
             arrive("g halo", k)
         scale = jnp.concatenate([es_f[rows_of(k), :]] * 2, axis=1)
         for group in range(OWN // 256 + k):
@@ -460,23 +488,20 @@
         if k == EARLY:
             send_rims(0, slice(EARLY * SLAB, LEV))
     send_rims(1, slice(0, EARLY * SLAB))
-    for k in range(last):
-        give_back("d", d_f, d_r, k, dr_send, dr_recv)
-    due_back("d", d_r, dr_send, dr_recv, me != last)
 
     every_row = slice(0, LEV)
-    inner = {c: transposed(every_row, c) for c in range(1, FOURS - 1)}
-    for c in inner:
-        i_f[:, (c + 1) * 256 : (c + 2) * 256] = inner[c].astype(BF16)
+    for c in range(1, FOURS - 1):
+        i_f[:, (c + 1) * 256 : (c + 2) * 256] = transposed(every_row, c).astype(BF16)
+    for n, c in enumerate(EDGES):
+        p_own[:, n * 256 : (n + 1) * 256] = transposed(every_row, c)
     build_turn()
     for k in range(WIN):
         arrive("dep", k)
     arrive("rims", 0)
     arrive("rims", 1)
-    for side, groups in ((0, (-1, 0)), (1, (FOURS - 1, FOURS))):
-        for n, c in enumerate(groups):
-            there = p_in[side, :, n * 256 : (n + 1) * 256].astype(F32)
-            i_f[:, (c + 1) * 256 : (c + 2) * 256] = (transposed(every_row, c) + there).astype(BF16)
+    for n, c in enumerate(EDGES):
+        there = p_in[n // 2, :, (n % 2) * 256 : (n % 2 + 1) * 256].astype(F32)
+        i_f[:, (c + 1) * 256 : (c + 2) * 256] = (p_own[:, n * 256 : (n + 1) * 256] + there).astype(BF16)
     scale = es_f[...]
     scale = jnp.concatenate([scale, scale], axis=1)
     for r in range(FOURS):
@@ -487,9 +512,14 @@
         value = dep_f[:, at].astype(F32) - scale * product
         t_own[:, at] = value
         t_f[:, HALO + r * 256 : HALO + (r + 1) * 256] = value.astype(BF16)
-
-    for k in range(WIN - 1):
-        start_sides(("t halo", k), halo_copies(t_f, k, HALO - TURN * k, th_send, th_recv))
+    for k in range(last):
+        give_back("d", d_f, d_r, k, dr_send, dr_recv)
+    due_back("d", d_r, dr_send, dr_recv, me != last)
+
+    for windows in T_GROUPS:
+        start_sides(
+            ("t halo", windows[0]), halo_copies(t_f, windows, HALO - TURN * windows[0], th_send, th_recv)
+        )
 
     def target(k, m):
         c = m - M_SIDE // 2
@@ -506,7 +536,7 @@
         x_f[rows_of(0), at] = t_f[rows_of(0), at]
         x_lo[rows_of(0), at] = jnp.zeros((SLAB, HALO), BF16)
     for k in range(1, WIN):
-        if k < WIN - 1:
+        if ("t halo", k) in due:
             arrive("t halo", k)
         for group in range(OWN // 256 + WIN - 1 - k):
             m = k + 2 * group
@@ -531,6 +561,9 @@
         d_r[...] = g_t[...]
 
     finish("d", d_r, d_out)
+    for wait in sent:
+        wait()
+    sent.clear()
     finish("x", x_r, x_out)
     close()
 
@@ -567,12 +600,14 @@
             vmem((LEV, 128), F32),
             vmem((LEV, EXT), BF16),
             vmem((LEV, OWN), BF16),
+            vmem((WIN, 1, LEV), F32),
             vmem((LEV, 128), F32),
             vmem((LEV, EXT), BF16),
             vmem((LEV, EXT), BF16),
             vmem((LEV, OWN), BF16),
             vmem((2, LEV, 2 * RIM), BF16),
             vmem((2, LEV, 2 * RIM), BF16),
+            vmem((LEV, 4 * RIM), F32),
             vmem((LEV, OWN + 2 * RIM), BF16),
             vmem((LEV, OWN), F32),
             vmem((LEV, EXT), BF16),

time: 44.5 us -> 42.2 us (0.948)
  Pallas kernels: 42.6 us -> 40.4 us
    pallas_call x1, Pallas kernels: 42.6 us -> 40.4 us  [body(): pl.pallas_call(functools.partial(kernel, ncol), out_shape=[pltpu.VMEM((OW...]
where the time goes in v3:
time: 42.2 us; the launch traced here: 42.1 us
  Pallas kernels  40.4 us (96%)
  other arithmetic  1.1 us (3%)
  between operations  0.67 us (2%)
    pallas_call x1, Pallas kernels, body(): pl.pallas_call(functools.partial(kernel, ncol), out_shape=[pltpu.VMEM((OW...  40.4 us
    add x1, other arithmetic, body(): dual_next = (1.0 - RELAX) * dual_field + RELAX * d_new.astype(F32)[None]  1.1 us

profile of v3, /device:TPU:6, one launch (start us, length us, event | category | flops | bytes accessed | tf_op | source)
XLA Modules:
  0.0 42.1 jit_solution(6044495242479558044)
XLA Ops:
  0.6 0.0 copy-start
  0.6 0.0 copy-start.1
  0.7 40.4 %shard_map.113 = (bf16[1024,128]{1,0:T(8,128)(2,1)S(1)}, bf16[1024,128]{1,0:T(8,128)(2,1)S(1)}) custom-call(f32[1,1024,128]{2,1,0:T(8,128)} %inc.1, f32[1,1024,128]{2,1,0:T(8,128)} %dep.1, f32[1,1024,128]{2,1,0:T(8,128)} %og.1, bf16[1,1024,128]{2,1,0:T(8,128)(2,1)} %ow.1, f32[1,128]{1,0:T(1,128)} %es.1, bf16[16,64,512]{2,1,0:T(8,128)(2,1)} %cb.1, ...), custom_call_target="tpu_custom_call" | custom-call | tf_op jit(solution)/shard_map/pallas_call | solution.py:587
  41.0 0.0 copy-done
  41.0 0.0 copy-done.1
  41.0 1.1 %bitcast_add_fusion = (f32[1,1024,128]{2,1,0:T(8,128)}, f32[1,1024,128]{2,1,0:T(8,128)}) fusion(bf16[1024,128]{1,0:T(8,128)(2,1)S(1)} %get-tuple-element.5, f32[1,1024,128]{2,1,0:T(8,128)S(1)} %copy-done.1, bf16[1024,128]{1,0:T(8,128)(2,1)S(1)} %get-tuple-element.4, f32[1,1024,128]{2,1,0:T(8,128)S(1)} %copy-done), kind=kLoop, calls=%fused_computation | loop fusion | flops 1048576 | bytes 2621440 | tf_op jit(solution)/shard_map/add | solution.py:649
Async XLA Ops:
  0.6 40.4 %copy-start = (f32[1,1024,128]{2,1,0:T(8,128)S(1)}, f32[1,1024,128]{2,1,0:T(8,128)}, u32[]{:S(2)}) copy-start(f32[1,1024,128]{2,1,0:T(8,128)} %inc.1) | copy-start | bytes 1572868
  0.6 40.4 %copy-start.1 = (f32[1,1024,128]{2,1,0:T(8,128)S(1)}, f32[1,1024,128]{2,1,0:T(8,128)}, u32[]{:S(2)}) copy-start(f32[1,1024,128]{2,1,0:T(8,128)} %param.11) | copy-start | bytes 1572868

commit v4 on v3

--- a/solution.py
+++ b/solution.py
@@ -25,6 +25,7 @@
 FOURS = OWN // 256
 EDGES = (-1, 0, FOURS - 1, FOURS)
 EARLY = 4
+HELD = (5, 3)
 G_GROUPS = ((6, 7), (3, 4, 5), (1, 2))
 T_GROUPS = ((0, 1), (2, 3), (4, 5, 6))
 RELAX = 0.75
@@ -546,6 +547,9 @@
             product = jnp.dot(field, weights(m_turn, m), preferred_element_type=F32)
             base = jnp.concatenate([target(k, m), target(k, m + 1)], axis=1)
             x_f[rows_of(k), at], x_lo[rows_of(k), at] = split(base + product[:SLAB] + product[SLAB:])
+        if k not in HELD:
+            give_back("x", x_f, x_r, k, xr_send, xr_recv)
+    for k in HELD:
         give_back("x", x_f, x_r, k, xr_send, xr_recv)
     due_back("x", x_r, xr_send, xr_recv, me >= 0)
 

time: 42.2 us -> 42.1 us (level)
  no operation moved by 1% of the time
where the time goes in v4:
time: 42.1 us; the launch traced here: 42 us
  Pallas kernels  40.2 us (95%)
  other arithmetic  1.1 us (3%)
  between operations  0.67 us (2%)
    pallas_call x1, Pallas kernels, body(): pl.pallas_call(functools.partial(kernel, ncol), out_shape=[pltpu.VMEM((OW...  40.2 us
    add x1, other arithmetic, body(): dual_next = (1.0 - RELAX) * dual_field + RELAX * d_new.astype(F32)[None]  1.1 us

profile of v4, /device:TPU:6, one launch (start us, length us, event | category | flops | bytes accessed | tf_op | source)
XLA Modules:
  0.0 42.0 jit_solution(2642292118345325469)
XLA Ops:
  0.6 0.0 copy-start
  0.6 0.0 copy-start.1
  0.7 40.2 %shard_map.113 = (bf16[1024,128]{1,0:T(8,128)(2,1)S(1)}, bf16[1024,128]{1,0:T(8,128)(2,1)S(1)}) custom-call(f32[1,1024,128]{2,1,0:T(8,128)} %inc.1, f32[1,1024,128]{2,1,0:T(8,128)} %dep.1, f32[1,1024,128]{2,1,0:T(8,128)} %og.1, bf16[1,1024,128]{2,1,0:T(8,128)(2,1)} %ow.1, f32[1,128]{1,0:T(1,128)} %es.1, bf16[16,64,512]{2,1,0:T(8,128)(2,1)} %cb.1, ...), custom_call_target="tpu_custom_call" | custom-call | tf_op jit(solution)/shard_map/pallas_call | solution.py:591
  40.9 0.0 copy-done
  40.9 0.0 copy-done.1
  40.9 1.1 %bitcast_add_fusion = (f32[1,1024,128]{2,1,0:T(8,128)}, f32[1,1024,128]{2,1,0:T(8,128)}) fusion(bf16[1024,128]{1,0:T(8,128)(2,1)S(1)} %get-tuple-element.5, f32[1,1024,128]{2,1,0:T(8,128)S(1)} %copy-done.1, bf16[1024,128]{1,0:T(8,128)(2,1)S(1)} %get-tuple-element.4, f32[1,1024,128]{2,1,0:T(8,128)S(1)} %copy-done), kind=kLoop, calls=%fused_computation | loop fusion | flops 1048576 | bytes 2621440 | tf_op jit(solution)/shard_map/add | solution.py:653
Async XLA Ops:
  0.6 40.3 %copy-start = (f32[1,1024,128]{2,1,0:T(8,128)S(1)}, f32[1,1024,128]{2,1,0:T(8,128)}, u32[]{:S(2)}) copy-start(f32[1,1024,128]{2,1,0:T(8,128)} %inc.1) | copy-start | bytes 1572868
  0.6 40.3 %copy-start.1 = (f32[1,1024,128]{2,1,0:T(8,128)S(1)}, f32[1,1024,128]{2,1,0:T(8,128)}, u32[]{:S(2)}) copy-start(f32[1,1024,128]{2,1,0:T(8,128)} %param.11) | copy-start | bytes 1572868

commit v5 on v4

--- a/solution.py
+++ b/solution.py
@@ -16,7 +16,8 @@
 RU, NNZ_U = 4, 8
 RM, NNZ_M = 2, 4
 TURN = RM * BLK
-HALO = (WIN - 1) * TURN
+ALONE = 3
+HALO = (WIN - 1 - ALONE) * TURN
 EXT = OWN + 2 * HALO
 END = HALO + OWN
 RIM = RU * BLK
@@ -26,8 +27,10 @@
 EDGES = (-1, 0, FOURS - 1, FOURS)
 EARLY = 4
 HELD = (5, 3)
-G_GROUPS = ((6, 7), (3, 4, 5), (1, 2))
-T_GROUPS = ((0, 1), (2, 3), (4, 5, 6))
+SIDE = HALO // 128
+TILES = OWN // 128
+G_GROUPS = (((5, 6, 7), 256), ((3, 4), 384), ((1, 2), 256))
+T_GROUPS = (((0, 1, 2), 256), ((3, 4), 384), ((5, 6), 256))
 RELAX = 0.75
 MESH = pl.DeviceIdType.MESH
 F32 = jnp.float32
@@ -154,6 +157,10 @@
     side_recv,
     gh_send,
     gh_recv,
+    dh_send,
+    dh_recv,
+    xh_send,
+    xh_recv,
     p_send,
     p_recv,
     th_send,
@@ -244,19 +251,32 @@
         for k in range(WIN):
             due[name, k] = lambda k=k: back(k)
 
-    def halo_copies(src, windows, width, sends, recvs):
+    def halo_copies(src, windows, first, end, sends, recvs):
         window = windows[0]
         rows = pl.ds(window * SLAB, len(windows) * SLAB)
+        n = end - first
         return (
             to_side(
-                src.at[rows, pl.ds(HALO, width)], src.at[rows, pl.ds(END, width)],
+                src.at[rows, pl.ds(HALO + first, n)], src.at[rows, pl.ds(END + first, n)],
                 sends.at[window, 0], recvs.at[window, 0], 0,
             ),
             to_side(
-                src.at[rows, pl.ds(END - width, width)], src.at[rows, pl.ds(HALO - width, width)],
+                src.at[rows, pl.ds(END - end, n)], src.at[rows, pl.ds(HALO - end, n)],
                 sends.at[window, 1], recvs.at[window, 1], 1,
             ),
         )
+
+    def turn_halo(name, src, window, turn, sends, recvs):
+        start_sides((name, window), halo_copies(src, (window,), TURN * turn, min(TURN * (turn + 2), HALO), sends, recvs))
+
+    def alone(turn):
+        return [SIDE + turn + 2 * group for group in range(TILES // 2 - turn)]
+
+    def rims_of(turn):
+        return [first + 2 * group for first in (SIDE - turn, SIDE + TILES - turn) for group in range(turn)]
+
+    def wide(reach):
+        return [SIDE - reach + 2 * group for group in range(TILES // 2 + reach)]
 
     def close():
         for key in list(due):
@@ -409,11 +429,6 @@
     side_pairs = M_SIDE // 2
     build_m(side_pairs, side_pairs + ROWS // 2)
     build_u()
-    for k in range(WIN - 1, -1, -1):
-        arrive("g", k)
-        for windows in G_GROUPS:
-            if k == windows[0]:
-                start_sides(("g halo", windows[-1]), halo_copies(g_f, windows, TURN * windows[-1], gh_send, gh_recv))
     for k in range(WIN):
         arrive("es", k)
     rows = jnp.concatenate([es_all[k] for k in range(WIN)] + [jnp.zeros((128 - WIN, LEV), F32)], axis=0)
@@ -421,6 +436,40 @@
     columns = es_t[rows_of(me), :]
     for k in range(WIN):
         es_f[rows_of(k), :] = jnp.broadcast_to(columns[:, k : k + 1], (SLAB, 128))
+    for field in (d_lo, x_lo):
+        for first in (0, END):
+            field[:, first : first + HALO] = jnp.zeros((LEV, HALO), BF16)
+    for k in range(WIN - 1, -1, -1):
+        arrive("g", k)
+        for windows, width in G_GROUPS:
+            if k == windows[0]:
+                start_sides(("g halo", windows[0]), halo_copies(g_f, windows, 0, width, gh_send, gh_recv))
+
+    def back(k, m):
+        at = slice(m * 128, (m + 2) * 128)
+        near = slice((m - 1) * 128, (m + 3) * 128)
+        if k + 1 < WIN - 1:
+            field = jnp.concatenate([d_f[rows_of(k + 1), near], d_lo[rows_of(k + 1), near]], axis=0)
+        else:
+            field = g_f[rows_of(k + 1), near]
+        product = jnp.dot(field, weights(m_band, m), preferred_element_type=F32)
+        if k + 1 < WIN - 1:
+            product = product[:SLAB] + product[SLAB:]
+        value = g_f[rows_of(k), at].astype(F32) + product
+        d_f[rows_of(k), at], d_lo[rows_of(k), at] = split(value)
+        value = (jnp.concatenate([es_f[rows_of(k), :]] * 2, axis=1) * value).astype(BF16)
+        for n in range(2):
+            c = m + n - SIDE
+            if 0 <= c < TILES:
+                s_f[rows_of(k), c * 128 : (c + 1) * 128] = value[:, n * 128 : (n + 1) * 128]
+
+    last = WIN - 1
+    for turn in range(1, ALONE + 1):
+        for m in alone(turn):
+            back(last - turn, m)
+        turn_halo("d halo", d_f, last - turn, turn, dh_send, dh_recv)
+    give_out("dep", dep_t, dep_f, whole, dep_send, dep_recv)
+    dep_f[rows_of(me), :] = dep_t[rows_of(me), :]
     arrive("pattern")
     store_positions(0)
     store_positions(2)
@@ -429,8 +478,6 @@
     build_m(0, side_pairs)
     build_m(side_pairs + ROWS // 2, M_PAIRS)
 
-    give_out("dep", dep_t, dep_f, whole, dep_send, dep_recv)
-    dep_f[rows_of(me), :] = dep_t[rows_of(me), :]
     def scaled(k):
         scale = jnp.concatenate([es_f[rows_of(k), :]] * 2, axis=1)
         return lambda value: (scale * value).astype(BF16)
@@ -457,38 +504,25 @@
             sent.append(copies[side].wait_send)
         due["rims", part] = lambda: [copy.wait_recv() for copy in copies]
 
-    last = WIN - 1
-    arrive("g halo", last)
-    d_f[rows_of(last), :] = g_f[rows_of(last), :]
     scale = scaled(last)
     for r in range(FOURS):
         s_f[rows_of(last), r * 256 : (r + 1) * 256] = scale(
             g_f[rows_of(last), HALO + r * 256 : HALO + (r + 1) * 256].astype(F32)
         )
-    for k in range(last - 1, -1, -1):
-        if ("g halo", k) in due:
-            arrive("g halo", k)
-        scale = jnp.concatenate([es_f[rows_of(k), :]] * 2, axis=1)
-        for group in range(OWN // 256 + k):
-            m = M_SIDE // 2 - k + 2 * group
-            at = slice(m * 128, (m + 2) * 128)
-            near = slice((m - 1) * 128, (m + 3) * 128)
-            field = d_f[rows_of(k + 1), near]
-            if k + 1 < last:
-                field = jnp.concatenate([field, d_lo[rows_of(k + 1), near]], axis=0)
-            product = jnp.dot(field, weights(m_band, m), preferred_element_type=F32)
-            if k + 1 < last:
-                product = product[:SLAB] + product[SLAB:]
-            value = g_f[rows_of(k), at].astype(F32) + product
-            d_f[rows_of(k), at], d_lo[rows_of(k), at] = split(value)
-            value = (scale * value).astype(BF16)
-            for n in range(2):
-                c = m + n - M_SIDE // 2
-                if 0 <= c < OWN // 128:
-                    s_f[rows_of(k), c * 128 : (c + 1) * 128] = value[:, n * 128 : (n + 1) * 128]
+    for windows, _ in G_GROUPS:
+        arrive("g halo", windows[0])
+    for turn in range(1, WIN):
+        k = last - turn
+        for m in rims_of(turn) if turn <= ALONE else wide(k):
+            back(k, m)
+        if turn <= ALONE:
+            arrive("d halo", k)
         if k == EARLY:
             send_rims(0, slice(EARLY * SLAB, LEV))
     send_rims(1, slice(0, EARLY * SLAB))
+    for k in range(last):
+        give_back("d", d_f, d_r, k, dr_send, dr_recv)
+    due_back("d", d_r, dr_send, dr_recv, me != last)
 
     every_row = slice(0, LEV)
     for c in range(1, FOURS - 1):
@@ -513,40 +547,42 @@
         value = dep_f[:, at].astype(F32) - scale * product
         t_own[:, at] = value
         t_f[:, HALO + r * 256 : HALO + (r + 1) * 256] = value.astype(BF16)
-    for k in range(last):
-        give_back("d", d_f, d_r, k, dr_send, dr_recv)
-    due_back("d", d_r, dr_send, dr_recv, me != last)
-
-    for windows in T_GROUPS:
-        start_sides(
-            ("t halo", windows[0]), halo_copies(t_f, windows, HALO - TURN * windows[0], th_send, th_recv)
-        )
+
+    for windows, width in T_GROUPS:
+        start_sides(("t halo", windows[0]), halo_copies(t_f, windows, 0, width, th_send, th_recv))
 
     def target(k, m):
-        c = m - M_SIDE // 2
-        if 0 <= c < OWN // 128:
+        c = m - SIDE
+        if 0 <= c < TILES:
             return t_own[rows_of(k), c * 128 : (c + 1) * 128]
         return t_f[rows_of(k), m * 128 : (m + 1) * 128].astype(F32)
 
-    for c in range(OWN // 128):
+    def fore(k, m):
+        at = slice(m * 128, (m + 2) * 128)
+        near = slice((m - 1) * 128, (m + 3) * 128)
+        field = jnp.concatenate([x_f[rows_of(k - 1), near], x_lo[rows_of(k - 1), near]], axis=0)
+        product = jnp.dot(field, weights(m_turn, m), preferred_element_type=F32)
+        base = jnp.concatenate([target(k, m), target(k, m + 1)], axis=1)
+        x_f[rows_of(k), at], x_lo[rows_of(k), at] = split(base + product[:SLAB] + product[SLAB:])
+
+    for c in range(TILES):
         at = slice(HALO + c * 128, HALO + (c + 1) * 128)
         x_f[rows_of(0), at], x_lo[rows_of(0), at] = split(t_own[rows_of(0), c * 128 : (c + 1) * 128])
+    for k in range(1, ALONE + 1):
+        for m in alone(k):
+            fore(k, m)
+        turn_halo("x halo", x_f, k, k, xh_send, xh_recv)
     give_back("x", x_f, x_r, 0, xr_send, xr_recv)
-    arrive("t halo", 0)
-    for at in (slice(0, HALO), slice(END, EXT)):
+    for windows, _ in T_GROUPS:
+        arrive("t halo", windows[0])
+    for first in (HALO - 2 * TURN, END):
+        at = slice(first, first + 2 * TURN)
         x_f[rows_of(0), at] = t_f[rows_of(0), at]
-        x_lo[rows_of(0), at] = jnp.zeros((SLAB, HALO), BF16)
     for k in range(1, WIN):
-        if ("t halo", k) in due:
-            arrive("t halo", k)
-        for group in range(OWN // 256 + WIN - 1 - k):
-            m = k + 2 * group
-            at = slice(m * 128, (m + 2) * 128)
-            near = slice((m - 1) * 128, (m + 3) * 128)
-            field = jnp.concatenate([x_f[rows_of(k - 1), near], x_lo[rows_of(k - 1), near]], axis=0)
-            product = jnp.dot(field, weights(m_turn, m), preferred_element_type=F32)
-            base = jnp.concatenate([target(k, m), target(k, m + 1)], axis=1)
-            x_f[rows_of(k), at], x_lo[rows_of(k), at] = split(base + product[:SLAB] + product[SLAB:])
+        for m in rims_of(k) if k <= ALONE else wide(last - k):
+            fore(k, m)
+        if k <= ALONE:
+            arrive("x halo", k)
         if k not in HELD:
             give_back("x", x_f, x_r, k, xr_send, xr_recv)
     for k in HELD:
@@ -632,7 +668,7 @@
         ]
         + [dma((WIN,))] * 10
         + [dma((3, 2))] * 2
-        + [dma((WIN, 2))] * 2
+        + [dma((WIN, 2))] * 6
         + [dma((2, 2))] * 2
         + [dma((WIN, 2))] * 2,
         compiler_params=pltpu.CompilerParams(

time: 42.1 us -> 42.6 us (1.012)
  Pallas kernels: 40.2 us -> 40.7 us
    pallas_call x1, Pallas kernels: 40.2 us -> 40.7 us  [body(): pl.pallas_call(functools.partial(kernel, ncol), out_shape=[pltpu.VMEM((OW...]
where the time goes in v5:
time: 42.6 us; the launch traced here: 42.5 us
  Pallas kernels  40.7 us (96%)
  other arithmetic  1.1 us (3%)
  between operations  0.67 us (2%)
    pallas_call x1, Pallas kernels, body(): pl.pallas_call(functools.partial(kernel, ncol), out_shape=[pltpu.VMEM((OW...  40.7 us
    add x1, other arithmetic, body(): dual_next = (1.0 - RELAX) * dual_field + RELAX * d_new.astype(F32)[None]  1.1 us

profile of v5, /device:TPU:6, one launch (start us, length us, event | category | flops | bytes accessed | tf_op | source)
XLA Modules:
  0.0 42.5 jit_solution(3810092266127094595)
XLA Ops:
  0.6 0.0 copy-start
  0.6 0.0 copy-start.1
  0.7 40.7 %shard_map.113 = (bf16[1024,128]{1,0:T(8,128)(2,1)S(1)}, bf16[1024,128]{1,0:T(8,128)(2,1)S(1)}) custom-call(f32[1,1024,128]{2,1,0:T(8,128)} %inc.1, f32[1,1024,128]{2,1,0:T(8,128)} %dep.1, f32[1,1024,128]{2,1,0:T(8,128)} %og.1, bf16[1,1024,128]{2,1,0:T(8,128)(2,1)} %ow.1, f32[1,128]{1,0:T(1,128)} %es.1, bf16[16,64,512]{2,1,0:T(8,128)(2,1)} %cb.1, ...), custom_call_target="tpu_custom_call" | custom-call | tf_op jit(solution)/shard_map/pallas_call | solution.py:627
  41.4 0.0 copy-done
  41.4 0.0 copy-done.1
  41.4 1.1 %bitcast_add_fusion = (f32[1,1024,128]{2,1,0:T(8,128)}, f32[1,1024,128]{2,1,0:T(8,128)}) fusion(bf16[1024,128]{1,0:T(8,128)(2,1)S(1)} %get-tuple-element.5, f32[1,1024,128]{2,1,0:T(8,128)S(1)} %copy-done.1, bf16[1024,128]{1,0:T(8,128)(2,1)S(1)} %get-tuple-element.4, f32[1,1024,128]{2,1,0:T(8,128)S(1)} %copy-done), kind=kLoop, calls=%fused_computation | loop fusion | flops 1048576 | bytes 2621440 | tf_op jit(solution)/shard_map/add | solution.py:689
Async XLA Ops:
  0.6 40.7 %copy-start = (f32[1,1024,128]{2,1,0:T(8,128)S(1)}, f32[1,1024,128]{2,1,0:T(8,128)}, u32[]{:S(2)}) copy-start(f32[1,1024,128]{2,1,0:T(8,128)} %inc.1) | copy-start | bytes 1572868
  0.6 40.7 %copy-start.1 = (f32[1,1024,128]{2,1,0:T(8,128)S(1)}, f32[1,1024,128]{2,1,0:T(8,128)}, u32[]{:S(2)}) copy-start(f32[1,1024,128]{2,1,0:T(8,128)} %param.11) | copy-start | bytes 1572868
